TPU v7x, 32 devices: a whole 2x2x4 slice. The times are simulated.
32 devices in a mesh: dp: 8 (over z, x), tensor: 4 (over y, core).
Axes of the slice: x: 2, y: 2, z: 4, core: 2. Of those that a mesh axis runs over, the one named last changes fastest.
Arguments:
- tokens: bfloat16 [1024, 2048], P('dp'), may hold values from -6 to 6
- segments: int32 [1024], replicated, may hold values from 0 to 2, as said below
- routes: int32 [1024, 8], P(('dp', 'tensor')), may hold values from 0 to 31, all different within a row; in each aligned block of 32 rows (0 to 31, 32 to 63, ...) at most 16 rows name the same one
- out_grad: bfloat16 [1024, 2048], P(('dp', 'tensor')), may hold values from -6 to 6
- norm_gain: bfloat16 [2048], replicated, may hold values from 0.5 to 1.5
- q_weight: bfloat16 [2048, 4096], P('dp', 'tensor'), may hold values from -0.125 to 0.125
- k_weight: bfloat16 [2048, 512], P('dp', 'tensor'), may hold values from -0.125 to 0.125
- v_weight: bfloat16 [2048, 512], P('dp', 'tensor'), may hold values from -0.125 to 0.125
- q_gain: bfloat16 [128], replicated, may hold values from 0.796875 to 1.59375
- k_gain: bfloat16 [128], replicated, may hold values from 0.796875 to 1.59375
- out_weight: bfloat16 [2048, 4096], P('dp', 'tensor'), may hold values from -0.75 to 0.75
- moe_gain: bfloat16 [2048], replicated, may hold values from 0.5 to 1.5
- router_weight: bfloat16 [2048, 32], replicated, may hold values from -0.0625 to 0.0625
- gate_weight: bfloat16 [32, 2048, 768], P(('dp', 'tensor')), may hold values from -0.125 to 0.125
- up_weight: bfloat16 [32, 2048, 768], P(('dp', 'tensor')), may hold values from -0.125 to 0.125
- down_weight: bfloat16 [32, 768, 2048], P(('dp', 'tensor')), may hold values from -0.875 to 0.875
Outputs:
- layer_out: bfloat16 [1024, 2048], P(('dp', 'tensor'))
- tokens_grad: float32 [1024, 2048], P(('dp', 'tensor'))
- norm_gain_grad: float32 [2048], replicated
- q_weight_grad: float32 [2048, 4096], P('dp', 'tensor')
- k_weight_grad: float32 [2048, 512], P('dp', 'tensor')
- v_weight_grad: float32 [2048, 512], P('dp', 'tensor')
- q_gain_grad: float32 [128], replicated
- k_gain_grad: float32 [128], replicated
- out_weight_grad: float32 [2048, 4096], P('dp', 'tensor')
- moe_gain_grad: float32 [2048], replicated
- router_weight_grad: float32 [2048, 32], replicated
- gate_weight_grad: float32 [32, 2048, 768], P(('dp', 'tensor'))
- up_weight_grad: float32 [32, 2048, 768], P(('dp', 'tensor'))
- down_weight_grad: float32 [32, 768, 2048], P(('dp', 'tensor'))
Inputs may be any that keep to these rules, and one draw needn't show every extreme that they name: `routes`: each row names 8 different experts; in every aligned block of 32 rows no expert is named by more than 16 rows. `segments`: document numbers never fall along the tokens; document 1 begins within the first 128 tokens and ends within the last 128; documents 0 and 2 are not empty.
All inputs are finite; a program needn't handle non-finite values.
Results may differ from a plain program's by a relative error of at most 0.025.
Values may be sent and summed in bfloat16 or wider, within the bound.
A program may use at most 192 MiB of HBM per device.

v0:
```python
import jax
import jax.numpy as jnp
from jax import lax
from jax.sharding import PartitionSpec as P

EPS = 1e-06
THETA = 1000000.0


def norm_rows(values, gain):
    return values * lax.rsqrt(jnp.mean(values * values, axis=-1, keepdims=True) + EPS) * gain


def rotary(values, cosine, sine_part):
    half_dim = values.shape[-1] // 2
    front_half = values[..., :half_dim]
    back_half = values[..., half_dim:]
    return jnp.concatenate(
        [front_half * cosine - back_half * sine_part, back_half * cosine + front_half * sine_part],
        axis=-1,
    )


def angles(positions, head_dim):
    half_dim = head_dim // 2
    frequency = THETA ** (-(jnp.arange(half_dim).astype(jnp.float32) * 2.0) / head_dim)
    rotation = positions.astype(jnp.float32)[:, None] * frequency[None, :]
    return (jnp.cos(rotation), jnp.sin(rotation))


def prepare(projected, q_gain, k_gain, cosine, sine_part, head_dim):
    tok_rows = projected.shape[0]
    query_width = projected.shape[1] - 2 * head_dim
    queries = projected[:, :query_width].reshape(tok_rows, query_width // head_dim, head_dim)
    keys_local = projected[:, query_width : query_width + head_dim]
    values_local = projected[:, query_width + head_dim :]
    queries = rotary(norm_rows(queries, q_gain), cosine[:, None, :], sine_part[:, None, :])
    keys_local = rotary(norm_rows(keys_local, k_gain), cosine, sine_part)
    return (queries, keys_local, values_local)


def swiglu(gate_in, up_in):
    return jax.nn.silu(gate_in) * up_in


def shards(
    tokens,
    segments,
    routes,
    out_grad,
    norm_gain,
    q_weight,
    k_weight,
    v_weight,
    q_gain,
    k_gain,
    out_weight,
    moe_gain,
    router_weight,
    gate_weight,
    up_weight,
    down_weight,
):
    head_dim = q_gain.shape[0]
    tok_rows = tokens.shape[0]
    model_width = tokens.shape[1]
    share_rows = out_grad.shape[0]
    all_tokens = segments.shape[0]
    expert_count = router_weight.shape[1]
    top_count = routes.shape[1]
    capacity = max(2, share_rows * top_count * 2 // expert_count)
    score_scale = head_dim ** (-0.5)
    first_row = lax.axis_index("dp") * tok_rows
    places = jnp.arange(all_tokens, dtype=jnp.int32)
    begins = jnp.concatenate([jnp.ones((1,), dtype=bool), segments[1:] != segments[:-1]])
    positions = places - lax.cummax(jnp.where(begins, places, 0), axis=0)
    local_positions = lax.dynamic_slice_in_dim(positions, first_row, tok_rows)
    local_docs = lax.dynamic_slice_in_dim(segments, first_row, tok_rows)
    query_places = first_row + jnp.arange(tok_rows, dtype=jnp.int32)
    cosine, sine_part = angles(local_positions, head_dim)
    weight_rows = (
        lax.all_gather(q_weight, "dp", axis=0, tiled=True),
        lax.all_gather(k_weight, "dp", axis=0, tiled=True),
        lax.all_gather(v_weight, "dp", axis=0, tiled=True),
        lax.all_gather(out_weight, "dp", axis=0, tiled=True),
    )
    input_weight = jnp.concatenate([weight_rows[0], weight_rows[1], weight_rows[2]], axis=1)
    output_weight = weight_rows[3]
    tokens_float = tokens.astype(jnp.float32)
    norm_gain_float = norm_gain.astype(jnp.float32)
    hidden = norm_rows(tokens_float, norm_gain_float).astype(jnp.bfloat16)
    projected = jnp.dot(hidden, input_weight, preferred_element_type=jnp.float32)

    def prepare_local(projected_in, qgain_in, kgain_in):
        return prepare(projected_in, qgain_in, kgain_in, cosine, sine_part, head_dim)

    prepared, prepare_back = jax.vjp(
        prepare_local, projected, q_gain.astype(jnp.float32), k_gain.astype(jnp.float32)
    )
    queries = prepared[0].astype(jnp.bfloat16)
    keys_local = prepared[1].astype(jnp.bfloat16)
    values_local = prepared[2].astype(jnp.bfloat16)
    local_heads = queries.shape[1]

    def visible(offset, length):
        key_places = offset + jnp.arange(length, dtype=jnp.int32)
        key_docs = lax.dynamic_slice_in_dim(segments, offset, length)
        return (key_places[None, :] <= query_places[:, None]) & (
            key_docs[None, :] == local_docs[:, None]
        )

    running_max = jnp.full((tok_rows, local_heads), -1e30, jnp.float32)
    key_piece = lax.all_gather(keys_local, "dp", axis=0, tiled=True)
    value_piece = lax.all_gather(values_local, "dp", axis=0, tiled=True)
    allowed = visible(jnp.int32(0), key_piece.shape[0])[:, None, :]
    scores = (
        jnp.einsum("thd,nd->thn", queries, key_piece, preferred_element_type=jnp.float32)
        * score_scale
    )
    scores = jnp.where(allowed, scores, -1e30)
    new_max = jnp.maximum(running_max, jnp.max(scores, axis=-1))
    soft_weights = jnp.where(allowed, jnp.exp(scores - new_max[:, :, None]), 0.0)
    softmax_mass = jnp.sum(soft_weights, axis=-1)
    weighted_sum = jnp.einsum(
        "thn,nd->thd",
        soft_weights.astype(jnp.bfloat16),
        value_piece,
        preferred_element_type=jnp.float32,
    )
    running_max, softmax_mass, weighted_sum = (new_max, softmax_mass, weighted_sum)
    head_out = weighted_sum / softmax_mass[:, :, None]
    log_total = running_max + jnp.log(softmax_mass)
    attended = head_out.astype(jnp.bfloat16).reshape(tok_rows, local_heads * head_dim)
    branch = lax.psum_scatter(
        jnp.einsum("tc,dc->td", attended, output_weight, preferred_element_type=jnp.float32).astype(
            jnp.bfloat16
        ),
        "tensor",
        scatter_dimension=0,
        tiled=True,
    ).astype(jnp.float32)
    tensor_lane = lax.axis_index("tensor")
    tokens_share = lax.dynamic_slice_in_dim(tokens_float, tensor_lane * share_rows, share_rows, 0)
    middle = tokens_share + branch
    normed_float, moe_norm_back = jax.vjp(norm_rows, middle, moe_gain.astype(jnp.float32))
    normed = normed_float.astype(jnp.bfloat16)
    logits = jnp.dot(normed, router_weight, preferred_element_type=jnp.float32)

    def gating(logit_rows):
        probabilities = jax.nn.softmax(logit_rows, axis=-1)
        chosen = jnp.take_along_axis(probabilities, routes, axis=1)
        return chosen / jnp.sum(chosen, axis=1, keepdims=True)

    gate_values, gating_back = jax.vjp(gating, logits)
    pair_routes = routes.reshape(-1)
    pair_count = pair_routes.shape[0]
    route_table = (
        pair_routes[:, None] == jnp.arange(expert_count, dtype=jnp.int32)[None, :]
    ).astype(jnp.int32)
    route_rank = jnp.sum(jnp.cumsum(route_table, axis=0) * route_table, axis=1) - 1
    slot_index = pair_routes * capacity + route_rank
    slot_owner = (
        jnp.full((expert_count * capacity,), pair_count, jnp.int32)
        .at[slot_index]
        .set(jnp.arange(pair_count, dtype=jnp.int32))
    )
    normed_padded = jnp.concatenate([normed, jnp.zeros((1, model_width), jnp.bfloat16)], axis=0)
    send_rows = normed_padded[slot_owner // top_count].reshape(expert_count, capacity, model_width)
    arrived = lax.all_to_all(send_rows, ("dp", "tensor"), split_axis=0, concat_axis=0, tiled=True)
    expert_inputs = arrived.reshape(-1, model_width)
    w_gate = gate_weight[0]
    w_up = up_weight[0]
    w_down = down_weight[0]
    gate_act = jnp.dot(expert_inputs, w_gate, preferred_element_type=jnp.float32)
    up_act = jnp.dot(expert_inputs, w_up, preferred_element_type=jnp.float32)
    inner_float, swiglu_back = jax.vjp(swiglu, gate_act, up_act)
    inner_act = inner_float.astype(jnp.bfloat16)
    produced = jnp.dot(inner_act, w_down, preferred_element_type=jnp.float32).astype(jnp.bfloat16)
    returned = lax.all_to_all(
        produced.reshape(expert_count, capacity, model_width),
        ("dp", "tensor"),
        split_axis=0,
        concat_axis=0,
        tiled=True,
    )
    picked = (
        returned.reshape(-1, model_width)[slot_index]
        .reshape(share_rows, top_count, model_width)
        .astype(jnp.float32)
    )
    layer_out = (middle + jnp.sum(gate_values[:, :, None] * picked, axis=1)).astype(jnp.bfloat16)
    grad_out = out_grad.astype(jnp.float32)
    grad_picked = (
        (gate_values[:, :, None] * grad_out[:, None, :])
        .astype(jnp.bfloat16)
        .reshape(pair_count, model_width)
    )
    grad_gates = jnp.sum(grad_out[:, None, :] * picked, axis=2)
    grad_padded = jnp.concatenate([grad_picked, jnp.zeros((1, model_width), jnp.bfloat16)], axis=0)
    grad_send = grad_padded[slot_owner].reshape(expert_count, capacity, model_width)
    grad_arrived = lax.all_to_all(
        grad_send, ("dp", "tensor"), split_axis=0, concat_axis=0, tiled=True
    ).reshape(-1, model_width)
    grad_inner = jnp.einsum("rd,fd->rf", grad_arrived, w_down, preferred_element_type=jnp.float32)
    grad_down = jnp.einsum("rf,rd->fd", inner_act, grad_arrived, preferred_element_type=jnp.float32)
    grad_gate_float, grad_up_float = swiglu_back(grad_inner)
    grad_gate_act = grad_gate_float.astype(jnp.bfloat16)
    grad_up_act = grad_up_float.astype(jnp.bfloat16)
    grad_gate_w = jnp.einsum(
        "rd,rf->df", expert_inputs, grad_gate_act, preferred_element_type=jnp.float32
    )
    grad_up_w = jnp.einsum(
        "rd,rf->df", expert_inputs, grad_up_act, preferred_element_type=jnp.float32
    )
    grad_inputs = jnp.einsum("rf,df->rd", grad_gate_act, w_gate, preferred_element_type=jnp.float32)
    grad_inputs = (
        grad_inputs + jnp.einsum("rf,df->rd", grad_up_act, w_up, preferred_element_type=jnp.float32)
    ).astype(jnp.bfloat16)
    grad_home = lax.all_to_all(
        grad_inputs.reshape(expert_count, capacity, model_width),
        ("dp", "tensor"),
        split_axis=0,
        concat_axis=0,
        tiled=True,
    )
    grad_normed = jnp.sum(
        grad_home.reshape(-1, model_width)[slot_index]
        .reshape(share_rows, top_count, model_width)
        .astype(jnp.float32),
        axis=1,
    )
    (grad_logit_float,) = gating_back(grad_gates)
    grad_logits = grad_logit_float.astype(jnp.bfloat16)
    grad_router = jnp.einsum("td,te->de", normed, grad_logits, preferred_element_type=jnp.float32)
    grad_normed = grad_normed + jnp.einsum(
        "te,de->td", grad_logits, router_weight, preferred_element_type=jnp.float32
    )
    grad_middle_part, grad_moe_gain = moe_norm_back(grad_normed)
    grad_middle = grad_out + grad_middle_part
    grad_branch = lax.all_gather(grad_middle.astype(jnp.bfloat16), "tensor", axis=0, tiled=True)
    again_rows = (
        lax.all_gather(q_weight, "dp", axis=0, tiled=True),
        lax.all_gather(k_weight, "dp", axis=0, tiled=True),
        lax.all_gather(v_weight, "dp", axis=0, tiled=True),
        lax.all_gather(out_weight, "dp", axis=0, tiled=True),
    )
    input_back = jnp.concatenate([again_rows[0], again_rows[1], again_rows[2]], axis=1)
    output_back = again_rows[3]
    grad_heads = (
        jnp.dot(grad_branch, output_back, preferred_element_type=jnp.float32)
        .astype(jnp.bfloat16)
        .reshape(tok_rows, local_heads, head_dim)
    )
    row_delta = jnp.sum(grad_heads.astype(jnp.float32) * head_out, axis=-1)
    key_rows, value_rows = (
        lax.all_gather(keys_local, "dp", axis=0, tiled=True),
        lax.all_gather(values_local, "dp", axis=0, tiled=True),
    )
    key_block = min(512, all_tokens)

    def key_step(grad_queries, block_number):
        offset = block_number * key_block
        key_piece = lax.dynamic_slice_in_dim(key_rows, offset, key_block, 0)
        value_piece = lax.dynamic_slice_in_dim(value_rows, offset, key_block, 0)
        allowed = visible(offset, key_block)[:, None, :]
        scores = (
            jnp.einsum("thd,nd->thn", queries, key_piece, preferred_element_type=jnp.float32)
            * score_scale
        )
        soft_weights = jnp.where(allowed, jnp.exp(scores - log_total[:, :, None]), 0.0)
        grad_weights = jnp.einsum(
            "thd,nd->thn", grad_heads, value_piece, preferred_element_type=jnp.float32
        )
        grad_scores = (soft_weights * (grad_weights - row_delta[:, :, None])).astype(jnp.bfloat16)
        grad_queries = (
            grad_queries
            + jnp.einsum("thn,nd->thd", grad_scores, key_piece, preferred_element_type=jnp.float32)
            * score_scale
        )
        grad_key_piece = (
            jnp.einsum("thn,thd->nd", grad_scores, queries, preferred_element_type=jnp.float32)
            * score_scale
        )
        grad_value_piece = jnp.einsum(
            "thn,thd->nd",
            soft_weights.astype(jnp.bfloat16),
            grad_heads,
            preferred_element_type=jnp.float32,
        )
        return (grad_queries, jnp.concatenate([grad_key_piece, grad_value_piece], axis=1))

    grad_queries, key_terms = lax.scan(
        key_step,
        jnp.zeros((tok_rows, local_heads, head_dim), jnp.float32),
        jnp.arange(all_tokens // key_block, dtype=jnp.int32),
    )
    key_grads = lax.psum_scatter(
        key_terms.reshape(all_tokens, 2 * head_dim).astype(jnp.bfloat16),
        "dp",
        scatter_dimension=0,
        tiled=True,
    ).astype(jnp.float32)
    grad_proj_float, grad_q_gain, grad_k_gain = prepare_back(
        (grad_queries, key_grads[:, :head_dim], key_grads[:, head_dim:])
    )
    grad_projected = grad_proj_float.astype(jnp.bfloat16)
    grad_hidden = jnp.einsum(
        "tc,dc->td", grad_projected, input_back, preferred_element_type=jnp.float32
    )
    grad_hidden_share = lax.psum_scatter(
        grad_hidden.astype(jnp.bfloat16), "tensor", scatter_dimension=0, tiled=True
    ).astype(jnp.float32)
    _, first_norm_back = jax.vjp(norm_rows, tokens_share, norm_gain_float)
    grad_tokens_part, grad_norm_gain = first_norm_back(grad_hidden_share)
    tokens_grad = grad_middle + grad_tokens_part
    input_part = jnp.einsum("td,tc->dc", hidden, grad_projected, preferred_element_type=jnp.float32)
    output_part = jnp.einsum("td,tc->dc", grad_branch, attended, preferred_element_type=jnp.float32)
    weight_share = lax.psum_scatter(
        jnp.concatenate([input_part, output_part], axis=1).astype(jnp.bfloat16),
        "dp",
        scatter_dimension=0,
        tiled=True,
    ).astype(jnp.float32)
    query_width = local_heads * head_dim
    grad_q_weight = weight_share[:, :query_width]
    grad_k_weight = weight_share[:, query_width : query_width + head_dim]
    grad_v_weight = weight_share[:, query_width + head_dim : query_width + 2 * head_dim]
    grad_out_weight = weight_share[:, query_width + 2 * head_dim :]
    small_sums = lax.psum(
        (grad_router, grad_norm_gain, grad_moe_gain, grad_q_gain, grad_k_gain), ("dp", "tensor")
    )
    return (
        layer_out,
        tokens_grad,
        small_sums[1],
        grad_q_weight,
        grad_k_weight,
        grad_v_weight,
        small_sums[3],
        small_sums[4],
        grad_out_weight,
        small_sums[2],
        small_sums[0],
        grad_gate_w[None],
        grad_up_w[None],
        grad_down[None],
    )


def solution(mesh):
    placed = (
        P("dp", None),
        P(),
        P(("dp", "tensor"), None),
        P(("dp", "tensor"), None),
        P(),
        P("dp", "tensor"),
        P("dp", "tensor"),
        P("dp", "tensor"),
        P(),
        P(),
        P("dp", "tensor"),
        P(),
        P(),
        P(("dp", "tensor"), None, None),
        P(("dp", "tensor"), None, None),
        P(("dp", "tensor"), None, None),
    )
    return jax.shard_map(
        shards,
        mesh=mesh,
        in_specs=placed,
        out_specs=(
            P(("dp", "tensor"), None),
            P(("dp", "tensor"), None),
            P(),
            P("dp", "tensor"),
            P("dp", "tensor"),
            P("dp", "tensor"),
            P(),
            P(),
            P("dp", "tensor"),
            P(),
            P(),
            P(("dp", "tensor"), None, None),
            P(("dp", "tensor"), None, None),
            P(("dp", "tensor"), None, None),
        ),
        check_vma=False,
    )
```

profile of v0, /device:TPU:0, one launch (start us, length us, event | category | flops | bytes accessed | tf_op | source)
XLA Modules:
  0.0 905.1 jit_solution(2913621800738254680)
XLA Ops:
  17.8 37.0 %all_gather.28 = bf16[2048,128]{1,0:T(8,128)(2,1)} all-gather(bf16[256,128]{1,0:T(8,128)(2,1)} %param.24), channel_id=1, replica_groups=mesh['dp'=8,'tensor'=4] {'dp'}, dimensions={0}, use_global_device_ids=true | all-gather | bytes 589824 | tf_op jit(solution)/shard_map/all_gather | solution.py:83
  54.8 35.1 %all_gather.29 = bf16[2048,128]{1,0:T(8,128)(2,1)} all-gather(bf16[256,128]{1,0:T(8,128)(2,1)} %param.25), channel_id=1, replica_groups=mesh['dp'=8,'tensor'=4] {'dp'}, dimensions={0}, use_global_device_ids=true | all-gather | bytes 589824 | tf_op jit(solution)/shard_map/all_gather | solution.py:84
  89.9 8.5 all-gather.3.cloned.1.call-done
  98.5 2.7 constant_dynamic-update-slice_fusion.2
  102.5 1.4 copy-done.2
  108.4 33.8 %all_gather.30 = bf16[1024,128]{1,0:T(8,128)(2,1)} all-gather(bf16[128,128]{1,0:T(8,128)(2,1)S(1)} %pad_maximum_fusion.2), channel_id=1, replica_groups=mesh['dp'=8,'tensor'=4] {'dp'}, dimensions={0}, use_global_device_ids=true | all-gather | bytes 294912 | tf_op jit(solution)/shard_map/all_gather | solution.py:113
  142.1 31.9 %all_gather.31 = bf16[1024,128]{1,0:T(8,128)(2,1)S(1)} all-gather(bf16[128,128]{1,0:T(8,128)(2,1)S(1)} %slice.123), channel_id=1, replica_groups=mesh['dp'=8,'tensor'=4] {'dp'}, dimensions={0}, use_global_device_ids=true | all-gather | bytes 294912 | tf_op jit(solution)/shard_map/all_gather | solution.py:114
  174.0 1.3 fusion.52
  176.5 1.9 fusion.16
  181.0 2.1 fusion.101
  183.1 4.6 convolution_convert_fusion.3
  187.8 2.1 convert_element_type.132
  192.8 1.9 scatter_custom_fusion
  195.2 12.9 %reduce-scatter.5.cloned.1.call-done = bf16[32,2048]{1,0:T(8,128)(2,1)} async-done(((bf16[128,2048]{1,0:T(8,128)(2,1)}), bf16[32,2048]{1,0:T(8,128)(2,1)}) %reduce-scatter.5.cloned.1.call-update) | async-done | bytes 131088 | tf_op jit(solution)/shard_map/reduce_scatter | solution.py:134
  208.1 1.7 multiply_reduce_fusion.7
  211.7 2.0 gather_fusion.4
  215.4 6.6 gather_fusion.2
  222.0 4.7 all-to-all-start.2
  226.8 3.3 gather_fusion
  230.1 45.4 %all-to-all-done.2 = bf16[32,16,2048]{2,1,0:T(8,128)(2,1)} async-done(((bf16[32,16,2048]{2,1,0:T(8,128)(2,1)}), bf16[32,16,2048]{2,1,0:T(8,128)(2,1)}, u32[]{:S(2)}, u32[]{:S(2)}) %all-to-all-start.2) | async-done | bytes 2097184 | tf_op jit(solution)/shard_map/all_to_all | solution.py:201
  275.5 4.2 all-to-all-start
  279.8 5.5 fusion.17
  285.2 43.3 %all-to-all-done = bf16[32,16,2048]{2,1,0:T(8,128)(2,1)} async-done(((bf16[32,16,2048]{2,1,0:T(8,128)(2,1)}), bf16[32,16,2048]{2,1,0:T(8,128)(2,1)}, u32[]{:S(2)}, u32[]{:S(2)}) %all-to-all-start) | async-done | bytes 2097184 | tf_op jit(solution)/shard_map/all_to_all | solution.py:169
  328.5 4.4 fusion.23
  333.0 5.1 fusion.44
  338.0 1.8 fusion.21
  339.9 3.2 add_convert_fusion
  343.0 4.1 all-to-all-start.3
  347.2 5.0 fusion.29
  352.2 43.7 %all-to-all-done.3 = bf16[32,16,2048]{2,1,0:T(8,128)(2,1)S(1)} async-done(((bf16[32,16,2048]{2,1,0:T(8,128)(2,1)}), bf16[32,16,2048]{2,1,0:T(8,128)(2,1)S(1)}, u32[]{:S(2)}, u32[]{:S(2)}) %all-to-all-start.3) | async-done | bytes 2097184 | tf_op jit(solution)/shard_map/all_to_all | solution.py:219
  395.9 4.2 all-to-all-start.1
  401.8 2.3 gather_fusion.3
  404.2 1.9 convert_reduce_fusion
  406.1 42.8 %all-to-all-done.1 = bf16[32,16,2048]{2,1,0:T(8,128)(2,1)} async-done(((bf16[32,16,2048]{2,1,0:T(8,128)(2,1)}), bf16[32,16,2048]{2,1,0:T(8,128)(2,1)}, u32[]{:S(2)}, u32[]{:S(2)}) %all-to-all-start.1) | async-done | bytes 2097184 | tf_op jit(solution)/shard_map/all_to_all | solution.py:179
  448.9 4.3 gather_fusion.1
  453.2 2.3 fusion.37
  455.9 12.9 %scatter_fusion = f32[32,32]{1,0:T(8,128)S(1)} fusion(f32[32,32]{1,0:T(8,128)S(1)} %broadcast_in_dim.139, s32[256]{0:T(256)S(1)} %reshape.504, f32[256]{0:T(256)S(1)} %reshape.506), kind=kCustom, calls=%fused_computation.6 | custom fusion | flops 256 | bytes 5120 | tf_op jit(solution)/shard_map/transpose(jvp(jit(take_along_axis)))/scatter-add | solution.py:151
  470.2 7.2 all_gather.33
  477.4 3.1 convolution_convert_fusion.4
  481.3 21.5 %while.13 = (s32[]{:T(128)}, f32[128,8,128]{2,0,1:T(8,128)}, bf16[2,512,256]{1,2,0:T(8,128)(2,1)}, s32[2]{0:T(128)}, s32[1024]{0:T(1024)S(1)}, /*index=5*/s32[12...) while((s32[]{:T(128)}, f32[128,8,128]{2,0,1:T(8,128)}, ...), condition=%wide.region_25.26_spmd.clone, body=%wide.region_24.25_spmd.clone.sunk | while | flops 676004480 | bytes 17059644 | solution.py:292
  484.1 1.5 bitcast_select_fusion.2
  487.0 2.2 fusion.163
  489.7 1.4 fusion.164
  494.7 1.5 bitcast_select_fusion.2
  497.6 2.4 fusion.163
  500.5 1.4 fusion.164
  502.8 2.1 copy.153
  505.2 1.5 multiply_add_fusion.1
  507.8 3.2 convolution_convert_fusion.1
  511.1 55.4 %reduce-scatter.7.cloned.1.call-done = bf16[128,256]{1,0:T(8,128)(2,1)} async-done(((bf16[1024,256]{1,0:T(8,128)(2,1)}), bf16[128,256]{1,0:T(8,128)(2,1)}) %reduce-scatter.7.cloned.1.call-update) | async-done | bytes 65552 | tf_op jit(solution)/shard_map/reduce_scatter | solution.py:297
  570.4 5.2 convolution_convert_fusion.2
  575.7 1.6 convolution_convert_fusion
  577.9 11.2 %pad_maximum_fusion = bf16[2048,2304]{0,1:T(8,128)(2,1)} fusion(bf16[2048,1024]{0,1:T(8,128)(2,1)S(1)} %copy-done.3, bf16[2048,1280]{0,1:T(8,128)(2,1)S(1)} %convolution_convert_fusion), kind=kLoop, calls=%fused_computation.31 | loop fusion | flops 18874368 | bytes 18874368 | tf_op jit(solution)/shard_map/concatenate | solution.py:319
  590.2 6.2 convolution_bitcast_fusion.4
  596.5 6.2 convolution_bitcast_fusion.3
  602.7 6.5 convolution_bitcast_fusion.2
  611.3 43.9 %all-reduce.9 = (f32[2048]{0:T(1024)}, f32[128]{0:T(128)}, f32[128]{0:T(128)}, f32[2048]{0:T(1024)}) all-reduce(f32[2048]{0:T(1024)S(1)} %get-tuple-element.266, f32[128]{0:T(128)S(1)} %get-tuple-element.264, f32[128]{0:T(128)S(1)} %get-tuple-element.270, f32[2048]{0:T(1024)S(1)} %copy-done.60), channel_id=1, replica_groups=mesh['dp'=8,'tensor'=4] {'dp','tensor'}, use_global_device_ids=true, to_apply=%region_33.34 | all-reduce | flops 4352 | bytes 34816 | tf_op jit(solution)/shard_map/psum | solution.py:329
  655.3 1.8 fusion.58
  657.1 107.9 %reduce-scatter.11.cloned.1.call-done = bf16[256,2304]{0,1:T(8,128)(2,1)} async-done(((bf16[2048,2304]{0,1:T(8,128)(2,1)}), bf16[256,2304]{0,1:T(8,128)(2,1)}) %reduce-scatter.11.cloned.1.call-update) | async-done | bytes 1179664 | tf_op jit(solution)/shard_map/reduce_scatter | solution.py:318
  765.0 2.8 fusion.99
  767.9 2.5 copy.157
  772.8 2.5 copy.160
  775.3 120.8 %all-reduce.12.cloned.1.call-done = f32[2048,32]{0,1:T(8,128)} async-done(((f32[2048,32]{0,1:T(8,128)}), f32[2048,32]{0,1:T(8,128)}) %all-reduce.12.cloned.1.call-update) | async-done | bytes 262160 | tf_op jit(solution)/shard_map/psum | solution.py:329
  896.1 1.7 copy.193
  (346 shorter events, 51.5 us)
Async XLA Ops:
  7.2 325.8 %copy-start = (bf16[1,2048,768]{2,1,0:T(8,128)(2,1)S(1)}, bf16[1,2048,768]{2,1,0:T(8,128)(2,1)}, u32[]{:S(2)}) copy-start(bf16[1,2048,768]{2,1,0:T(8,128)(2,1)} %param.31) | copy-start | bytes 9437188
  7.2 91.3 %all-gather.3.cloned.1.call-start = ((), (), s32[]{:S(2)}) async-start(), calls=%async_computation.8 | async-start | bytes 4718592 | tf_op jit(solution)/shard_map/all_gather | solution.py:82
  7.9 175.1 %all-gather.5.cloned.1.call-start = ((), (), s32[]{:S(2)}) async-start(), calls=%async_computation.9 | async-start | bytes 4718592 | tf_op jit(solution)/shard_map/all_gather | solution.py:85
  8.7 199.5 %reduce-scatter.5.cloned.1.call-start = ((), (), s32[]{:S(2)}) async-start(), calls=%async_computation.10 | async-start | bytes 655360 | tf_op jit(solution)/shard_map/reduce_scatter | solution.py:134
  9.4 92.1 %copy-start.40 = (f32[2048]{0:T(1024)}, f32[2048]{0:T(1024)S(1)}, u32[]{:S(2)}) copy-start(f32[2048]{0:T(1024)S(1)} %convert_element_type.133) | copy-start | bytes 24580
  12.2 94.8 %copy-start.70 = (f32[128]{0:T(128)}, f32[128]{0:T(128)S(1)}, u32[]{:S(2)}) copy-start(f32[128]{0:T(128)S(1)} %convert_element_type.138) | copy-start | bytes 1540
  13.3 160.8 %copy-start.74 = (f32[128]{0:T(128)}, f32[128]{0:T(128)S(1)}, u32[]{:S(2)}) copy-start(f32[128]{0:T(128)S(1)} %convert_element_type.135) | copy-start | bytes 1540
  14.1 93.8 %copy-start.87 = (f32[64]{0:T(128)}, f32[64]{0:T(128)S(1)}, u32[]{:S(2)}) copy-start(f32[64]{0:T(128)S(1)} %multiply_power_fusion) | copy-start | bytes 772
  14.4 93.5 %copy-start.89 = (f32[128]{0:T(128)}, f32[128]{0:T(128)S(1)}, u32[]{:S(2)}) copy-start(f32[128]{0:T(128)S(1)} %dynamic-slice_convert_fusion) | copy-start | bytes 1540
  15.7 85.8 %copy-start.72 = (f32[128]{0:T(128)}, f32[128]{0:T(128)S(1)}, u32[]{:S(2)}) copy-start(f32[128]{0:T(128)S(1)} %add_rsqrt_fusion) | copy-start | bytes 1540
  105.9 72.5 %copy-start.56 = (f32[128,8]{0,1:T(8,128)}, f32[128,8]{0,1:T(8,128)S(1)}, u32[]{:S(2)}) copy-start(f32[128,8]{0,1:T(8,128)S(1)} %copy.139) | copy-start | bytes 12292
  106.9 71.5 %copy-start.91 = (f32[128]{0:T(128)}, f32[128]{0:T(128)S(1)}, u32[]{:S(2)}) copy-start(f32[128]{0:T(128)S(1)} %multiply_reduce_fusion.10) | copy-start | bytes 1540
  107.0 71.5 %copy-start.76 = (f32[128]{0:T(128)}, f32[128]{0:T(128)S(1)}, u32[]{:S(2)}) copy-start(f32[128]{0:T(128)S(1)} %fusion.91) | copy-start | bytes 1540
  108.2 67.4 %copy-start.32 = (f32[128,64]{1,0:T(8,128)}, f32[128,64]{1,0:T(8,128)S(1)}, u32[]{:S(2)}) copy-start(f32[128,64]{1,0:T(8,128)S(1)} %get-tuple-element.330) | copy-start | bytes 98308
  108.3 67.4 %copy-start.33 = (f32[128,64]{1,0:T(8,128)}, f32[128,64]{1,0:T(8,128)S(1)}, u32[]{:S(2)}) copy-start(f32[128,64]{1,0:T(8,128)S(1)} %get-tuple-element.331) | copy-start | bytes 98308
  183.1 6.8 copy-start.25
  183.1 6.9 copy-start.82
  183.1 7.9 copy-start.55
  183.1 8.1 copy-start.48
  190.0 21.2 %copy-start.44 = (f32[2048]{0:T(1024)}, f32[2048]{0:T(1024)S(1)}, u32[]{:S(2)}) copy-start(f32[2048]{0:T(1024)S(1)} %convert_element_type.143) | copy-start | bytes 24580
  190.9 23.2 %copy-start.19 = (f32[32,2048]{1,0:T(8,128)}, f32[32,2048]{1,0:T(8,128)S(1)}, u32[]{:S(2)}) copy-start(f32[32,2048]{1,0:T(8,128)S(1)} %convert_element_type.151) | copy-start | bytes 786436
  213.8 8.2 copy-start.42
  213.9 8.1 copy-start.78
  222.0 53.5 %all-to-all-start.2 = ((bf16[32,16,2048]{2,1,0:T(8,128)(2,1)}), bf16[32,16,2048]{2,1,0:T(8,128)(2,1)}, u32[]{:S(2)}, u32[]{:S(2)}) async-start(bf16[32,16,2048]{2,1,0:T(8,128)(2,1)} %bitcast.209), calls=%async_computation.3 | async-start | bytes 4194304 | tf_op jit(solution)/shard_map/all_to_all | solution.py:201
  275.5 53.0 %all-to-all-start = ((bf16[32,16,2048]{2,1,0:T(8,128)(2,1)}), bf16[32,16,2048]{2,1,0:T(8,128)(2,1)}, u32[]{:S(2)}, u32[]{:S(2)}) async-start(bf16[32,16,2048]{2,1,0:T(8,128)(2,1)} %bitcast.210), calls=%async_computation.1 | async-start | bytes 4194304 | tf_op jit(solution)/shard_map/all_to_all | solution.py:169
  343.0 52.9 %all-to-all-start.3 = ((bf16[32,16,2048]{2,1,0:T(8,128)(2,1)}), bf16[32,16,2048]{2,1,0:T(8,128)(2,1)S(1)}, u32[]{:S(2)}, u32[]{:S(2)}) async-start(bf16[32,16,2048]{2,1,0:T(8,128)(2,1)} %bitcast.212), calls=%async_computation.4 | async-start | bytes 4194304 | tf_op jit(solution)/shard_map/all_to_all | solution.py:219
  352.2 48.1 %copy-start.54 = (s32[32,8,1]{1,0,2:T(8,128)S(1)}, s32[32,8,1]{1,0,2:T(8,128)}, u32[]{:S(2)}) copy-start(s32[32,8,1]{1,0,2:T(8,128)} %get-tuple-element.326) | copy-start | bytes 3076
  352.2 48.2 %copy-start.84 = (s32[256,1]{0,1:T(1,128)S(1)}, s32[256,1]{0,1:T(1,128)}, u32[]{:S(2)}) copy-start(s32[256,1]{0,1:T(1,128)} %copy-done.83) | copy-start | bytes 3076
  352.2 48.2 %copy-start.18 = (bf16[128,8,128]{2,0,1:T(8,128)(2,1)S(1)}, bf16[128,8,128]{2,0,1:T(8,128)(2,1)}, u32[]{:S(2)}) copy-start(bf16[128,8,128]{2,0,1:T(8,128)(2,1)} %copy-done.17) | copy-start | bytes 786436
  352.2 49.0 %copy-start.59 = (f32[128,8]{0,1:T(8,128)S(1)}, f32[128,8]{0,1:T(8,128)}, u32[]{:S(2)}) copy-start(f32[128,8]{0,1:T(8,128)} %copy-done.58) | copy-start | bytes 12292
  352.2 49.0 %copy-start.63 = (f32[128,8]{0,1:T(8,128)S(1)}, f32[128,8]{0,1:T(8,128)}, u32[]{:S(2)}) copy-start(f32[128,8]{0,1:T(8,128)} %copy-done.62) | copy-start | bytes 12292
  352.2 49.6 %copy-start.79 = (f32[32]{0:T(128)S(1)}, f32[32]{0:T(128)}, u32[]{:S(2)}) copy-start(f32[32]{0:T(128)} %copy-done.78) | copy-start | bytes 388
  352.2 49.6 %copy-start.81 = (f32[32]{0:T(128)S(1)}, f32[32]{0:T(128)}, u32[]{:S(2)}) copy-start(f32[32]{0:T(128)} %copy-done.80) | copy-start | bytes 388
  395.9 53.0 %all-to-all-start.1 = ((bf16[32,16,2048]{2,1,0:T(8,128)(2,1)}), bf16[32,16,2048]{2,1,0:T(8,128)(2,1)}, u32[]{:S(2)}, u32[]{:S(2)}) async-start(bf16[32,16,2048]{2,1,0:T(8,128)(2,1)} %bitcast.211), calls=%async_computation.2 | async-start | bytes 4194304 | tf_op jit(solution)/shard_map/all_to_all | solution.py:179
  400.2 166.2 %reduce-scatter.7.cloned.1.call-start = ((), (), s32[]{:S(2)}) async-start(), calls=%async_computation.11 | async-start | bytes 589824 | tf_op jit(solution)/shard_map/reduce_scatter | solution.py:297
  455.8 13.0 %copy-start.39 = (f32[32,32]{0,1:T(8,128)S(1)}, f32[32,32]{0,1:T(8,128)}, u32[]{:S(2)}) copy-start(f32[32,32]{0,1:T(8,128)} %copy-done.38) | copy-start | bytes 12292
  455.8 13.0 %copy-start.65 = (f32[32]{0:T(128)S(1)}, f32[32]{0:T(128)}, u32[]{:S(2)}) copy-start(f32[32]{0:T(128)} %copy-done.64) | copy-start | bytes 388
  455.9 13.1 %copy-start.8 = (f32[32,2048]{1,0:T(8,128)S(1)}, f32[32,2048]{1,0:T(8,128)}, u32[]{:S(2)}) copy-start(f32[32,2048]{1,0:T(8,128)} %copy-done.7) | copy-start | bytes 786436
  455.9 13.1 %copy-start.37 = (bf16[2048,32]{0,1:T(8,128)(2,1)S(1)}, bf16[2048,32]{0,1:T(8,128)(2,1)}, u32[]{:S(2)}) copy-start(bf16[2048,32]{0,1:T(8,128)(2,1)} %param.30) | copy-start | bytes 393220
  455.9 13.1 %copy-start.45 = (f32[2048]{0:T(1024)S(1)}, f32[2048]{0:T(1024)}, u32[]{:S(2)}) copy-start(f32[2048]{0:T(1024)} %copy-done.44) | copy-start | bytes 24580
  455.9 13.1 %copy-start.68 = (f32[32]{0:T(128)S(1)}, f32[32]{0:T(128)}, u32[]{:S(2)}) copy-start(f32[32]{0:T(128)} %copy-done.67) | copy-start | bytes 388
  455.9 14.1 %copy-start.95 = (f32[32]{0:T(128)S(1)}, f32[32]{0:T(128)}, u32[]{:S(2)}) copy-start(f32[32]{0:T(128)} %copy-done.94) | copy-start | bytes 388
  455.9 14.1 %copy-start.27 = (bf16[32,2048]{1,0:T(8,128)(2,1)S(1)}, bf16[32,2048]{1,0:T(8,128)(2,1)}, u32[]{:S(2)}) copy-start(bf16[32,2048]{1,0:T(8,128)(2,1)} %param.21) | copy-start | bytes 393220
  469.0 11.5 %copy-start.50 = (bf16[32,32]{0,1:T(8,128)(2,1)}, bf16[32,32]{0,1:T(8,128)(2,1)S(1)}, u32[]{:S(2)}) copy-start(bf16[32,32]{0,1:T(8,128)(2,1)S(1)} %multiply_convert_fusion.6) | copy-start | bytes 6148
  470.0 10.5 %copy-start.15 = (f32[32,2048]{1,0:T(8,128)}, f32[32,2048]{1,0:T(8,128)S(1)}, u32[]{:S(2)}) copy-start(f32[32,2048]{1,0:T(8,128)S(1)} %get-tuple-element.338) | copy-start | bytes 786436
  470.0 10.5 %copy-start.85 = (f32[32]{0:T(128)}, f32[32]{0:T(128)S(1)}, u32[]{:S(2)}) copy-start(f32[32]{0:T(128)S(1)} %multiply_multiply_fusion.4) | copy-start | bytes 388
  470.1 10.6 %copy-start.34 = (f32[128,8,128]{0,2,1:T(8,128)S(1)}, f32[128,8,128]{0,2,1:T(8,128)}, u32[]{:S(2)}) copy-start(f32[128,8,128]{0,2,1:T(8,128)} %get-tuple-element.335) | copy-start | bytes 1572868
  504.9 105.2 %reduce-scatter.9.cloned.1.call-start = ((), (), s32[]{:S(2)}) async-start(), calls=%async_computation.12 | async-start | bytes 655360 | tf_op jit(solution)/shard_map/reduce_scatter | solution.py:310
  507.8 59.5 %copy-start.88 = (f32[64]{0:T(128)S(1)}, f32[64]{0:T(128)}, u32[]{:S(2)}) copy-start(f32[64]{0:T(128)} %copy-done.87) | copy-start | bytes 772
  507.8 59.5 %copy-start.90 = (f32[128]{0:T(128)S(1)}, f32[128]{0:T(128)}, u32[]{:S(2)}) copy-start(f32[128]{0:T(128)} %copy-done.89) | copy-start | bytes 1540
  507.8 59.8 %copy-start.71 = (f32[128]{0:T(128)S(1)}, f32[128]{0:T(128)}, u32[]{:S(2)}) copy-start(f32[128]{0:T(128)} %copy-done.70) | copy-start | bytes 1540
  507.8 59.8 %copy-start.77 = (f32[128]{0:T(128)S(1)}, f32[128]{0:T(128)}, u32[]{:S(2)}) copy-start(f32[128]{0:T(128)} %copy-done.76) | copy-start | bytes 1540
  507.8 60.9 %copy-start.92 = (f32[128]{0:T(128)S(1)}, f32[128]{0:T(128)}, u32[]{:S(2)}) copy-start(f32[128]{0:T(128)} %copy-done.91) | copy-start | bytes 1540
  575.6 189.4 %reduce-scatter.11.cloned.1.call-start = ((), (), s32[]{:S(2)}) async-start(), calls=%async_computation.13 | async-start | bytes 10616832 | tf_op jit(solution)/shard_map/reduce_scatter | solution.py:318
  589.1 307.0 %all-reduce.12.cloned.1.call-start = ((), (), s32[]{:S(2)}) async-start(), calls=%async_computation.14 | async-start | bytes 524288 | tf_op jit(solution)/shard_map/psum | solution.py:329
  602.7 7.5 copy-start.14
  602.7 8.6 copy-start.60
  602.7 52.6 %copy-start.9 = (f32[32,2048]{1,0:T(8,128)S(1)}, f32[32,2048]{1,0:T(8,128)}, u32[]{:S(2)}) copy-start(f32[32,2048]{1,0:T(8,128)} %copy-done.7) | copy-start | bytes 786436
  602.7 52.6 %copy-start.16 = (f32[32,2048]{1,0:T(8,128)S(1)}, f32[32,2048]{1,0:T(8,128)}, u32[]{:S(2)}) copy-start(f32[32,2048]{1,0:T(8,128)} %copy-done.15) | copy-start | bytes 786436
  602.7 52.6 %copy-start.28 = (bf16[32,2048]{1,0:T(8,128)(2,1)S(1)}, bf16[32,2048]{1,0:T(8,128)(2,1)}, u32[]{:S(2)}) copy-start(bf16[32,2048]{1,0:T(8,128)(2,1)} %param.21) | copy-start | bytes 393220
  602.7 52.5 %copy-start.29 = (f32[32,2048]{1,0:T(8,128)S(1)}, f32[32,2048]{1,0:T(8,128)}, u32[]{:S(2)}) copy-start(f32[32,2048]{1,0:T(8,128)} %get-tuple-element.269) | copy-start | bytes 786436
  602.7 52.5 %copy-start.69 = (f32[32]{0:T(128)S(1)}, f32[32]{0:T(128)}, u32[]{:S(2)}) copy-start(f32[32]{0:T(128)} %copy-done.67) | copy-start | bytes 388
  602.7 52.5 %copy-start.86 = (f32[32]{0:T(128)S(1)}, f32[32]{0:T(128)}, u32[]{:S(2)}) copy-start(f32[32]{0:T(128)} %copy-done.85) | copy-start | bytes 388
  765.0 132.8 %copy-start.1 = (bf16[1,2048,768]{2,1,0:T(8,128)(2,1)S(1)}, bf16[1,2048,768]{2,1,0:T(8,128)(2,1)}, u32[]{:S(2)}) copy-start(bf16[1,2048,768]{2,1,0:T(8,128)(2,1)} %param.31) | copy-start | bytes 9437188
  (51 other events, 158.5 us)
Sparse Core Ops, SparseCore 0:
  10.2 88.2 all-gather.2
  100.6 79.0 all-gather.4
  187.9 20.2 reduce-scatter.4
  505.0 61.3 reduce-scatter.6
  575.7 20.6 reduce-scatter.8
  600.3 164.6 reduce-scatter.10
  772.0 124.0 all-reduce.11
where the time goes:
time: 915 us; the launch traced here: 905 us
  waiting for transfers between devices  482 us (53%)
  blocking collectives  189 us (21%)
  matrix products  83.7 us (9%)
  other arithmetic  58.6 us (6%)
  local copies, waits for them, and re-layouts  56.1 us (6%)
  starting transfers between devices  18 us (2%)
  between operations  16 us (2%)
    psum x1, waiting for transfers between devices, shards(): lax.psum((grad_router, grad_norm_gain, grad_moe_gain, grad_q_gain, grad_k...  121 us
    reduce_scatter x1, waiting for transfers between devices, shards(): lax.psum_scatter(jnp.concatenate([input_part, output_part], axis=1).astyp...  108 us
    reduce_scatter x1, waiting for transfers between devices, shards(): lax.psum_scatter(key_terms.reshape(all_tokens, 2 * head_dim).astype(jnp.b...  55.4 us
    all_to_all x1, waiting for transfers between devices, shards(): lax.all_to_all(grad_send, ('dp', 'tensor'), split_axis=0, concat_axis=0,...  45.4 us
    psum x1, blocking collectives, shards(): lax.psum((grad_router, grad_norm_gain, grad_moe_gain, grad_q_gain, grad_k...  43.9 us
    all_to_all x1, waiting for transfers between devices, shards(): lax.all_to_all(grad_inputs.reshape(expert_count, capacity, model_width),...  43.7 us
    all_to_all x1, waiting for transfers between devices, shards(): lax.all_to_all(send_rows, ('dp', 'tensor'), split_axis=0, concat_axis=0,...  43.3 us
    all_to_all x1, waiting for transfers between devices, shards(): lax.all_to_all(produced.reshape(expert_count, capacity, model_width), ('d...  42.8 us
  transfers between devices with their start and end apart: 11, of which 9 were waited for; matrix products, arithmetic and copies ran while one was open for 11% of the time, Pallas kernels for 0%

commit v1 on v0

--- a/solution.py
+++ b/solution.py
@@ -1,6 +1,10 @@
+import functools
+
 import jax
 import jax.numpy as jnp
 from jax import lax
+from jax.experimental import pallas as pl
+from jax.experimental.pallas import tpu as pltpu
 from jax.sharding import PartitionSpec as P
 
 EPS = 1e-06
@@ -347,7 +351,697 @@
     )
 
 
+MESH = pl.DeviceIdType.MESH
+HBM = pl.ANY
+
+
+class Place:
+    def __init__(self, depth):
+        d = lax.axis_index("dp")
+        t = lax.axis_index("tensor")
+        self.depth = depth
+        self.d, self.t = d, t
+        self.z, self.x = d // 2, lax.rem(d, 2)
+        self.y, self.c = t // 2, lax.rem(t, 2)
+        self.next_to = {
+            "x": (self.z * 2 + 1 - self.x, t),
+            "y": (d, (1 - self.y) * 2 + self.c),
+            "c": (d, self.y * 2 + 1 - self.c),
+            "up": (d + 2, t),
+            "down": (d - 2, t),
+        }
+
+    def block(self, z, fx=0, fy=0, fc=0):
+        x = 1 - self.x if fx else self.x
+        y = 1 - self.y if fy else self.y
+        c = 1 - self.c if fc else self.c
+        return (z * 2 + x) * 4 + y * 2 + c
+
+    def at(self, dist, step):
+        if dist == 0:
+            step(self.z)
+            return
+
+        @pl.when(self.z >= dist)
+        def _():
+            step(self.z - dist)
+
+        @pl.when(self.z + dist < self.depth)
+        def _():
+            step(self.z + dist)
+
+    def greet(self):
+        barrier = pltpu.get_barrier_semaphore()
+
+        def signal(to):
+            pl.semaphore_signal(barrier, inc=1, device_id=self.next_to[to], device_id_type=MESH)
+
+        for to in ("x", "y", "c"):
+            signal(to)
+
+        @pl.when(self.z > 0)
+        def _():
+            signal("down")
+
+        @pl.when(self.z < self.depth - 1)
+        def _():
+            signal("up")
+
+        above = (self.z < self.depth - 1).astype(jnp.int32)
+        below = (self.z > 0).astype(jnp.int32)
+        pl.semaphore_wait(barrier, 3 + above + below)
+
+    def copy(self, src, dst, send, recv, to):
+        return pltpu.make_async_remote_copy(
+            src_ref=src,
+            dst_ref=dst,
+            send_sem=send,
+            recv_sem=recv,
+            device_id=self.next_to[to],
+            device_id_type=MESH,
+        )
+
+
+class Gather:
+    SEND, RECV = 11, 10
+
+    def __init__(self, pos, own, out, send, recv, halves):
+        self.pos, self.own, self.out = pos, own, out
+        self.send, self.recv = send, recv
+        rows = out.shape[1]
+        self.h0 = pl.ds(0, rows // 2 if halves else rows)
+        self.h1 = pl.ds(rows // 2, rows // 2) if halves else None
+        self.rounds = pos.depth + 2
+
+    def link(self, src, dst, sends, recvs, zo, to):
+        return self.pos.copy(src, dst, self.send.at[sends, zo], self.recv.at[recvs, zo], to)
+
+    def col(self, zo):
+        return self.out.at[self.pos.block(zo)]
+
+    def src(self, zo, mine):
+        return self.own if mine else self.col(zo)
+
+    def up(self, zo, mine=False):
+        return self.link(self.src(zo, mine), self.col(zo), 0, 0, zo, "up")
+
+    def down(self, zo, mine=False):
+        return self.link(self.src(zo, mine), self.col(zo), 1, 0, zo, "down")
+
+    def to_x(self, zo, mine=False):
+        return self.link(self.src(zo, mine), self.col(zo), 2, 1, zo, "x")
+
+    def to_y(self, zo, mine=False):
+        return self.link(self.src(zo, mine), self.col(zo), 3, 2, zo, "y")
+
+    def to_c(self, zo, mine=False):
+        return self.link(self.src(zo, mine), self.col(zo), 4, 5, zo, "c")
+
+    def part(self, zo, fx, fy, rows):
+        whole = self.out.at[self.pos.block(zo, fx, fy)]
+        return whole if rows is None else whole.at[rows]
+
+    def pass_on(self, zo, fx, fy, rows, sends, recvs, to):
+        ref = self.part(zo, fx, fy, rows)
+        return self.link(ref, ref, sends, recvs, zo, to)
+
+    def x_to_y(self, zo):
+        return self.pass_on(zo, 1, 0, self.h0, 5, 3, "y")
+
+    def x_to_c(self, zo):
+        return self.pass_on(zo, 1, 0, None, 6, 6, "c")
+
+    def y_to_x(self, zo):
+        return self.pass_on(zo, 0, 1, self.h1, 7, 4, "x")
+
+    def y_to_c(self, zo):
+        return self.pass_on(zo, 0, 1, None, 8, 7, "c")
+
+    def far0_to_c(self, zo):
+        return self.pass_on(zo, 1, 1, self.h0, 9, 8, "c")
+
+    def far1_to_c(self, zo):
+        return self.pass_on(zo, 1, 1, self.h1, 10, 9, "c")
+
+    def along_z(self, zo, mine, what):
+        z, depth = self.pos.z, self.pos.depth
+        if mine:
+            up, down = z < depth - 1, z > 0
+        else:
+            up, down = (zo < z) & (z < depth - 1), (zo > z) & (z > 0)
+
+        @pl.when(up)
+        def _():
+            what(self.up(zo, mine))
+
+        @pl.when(down)
+        def _():
+            what(self.down(zo, mine))
+
+    def on_column(self, zo, mine=False):
+        if not mine:
+            self.up(zo).wait_recv()
+        self.along_z(zo, mine, lambda c: c.start())
+        self.to_x(zo, mine).start()
+        self.to_y(zo, mine).start()
+        self.to_c(zo, mine).start()
+
+    def on_sides(self, zo):
+        self.to_x(zo).wait_recv()
+        self.x_to_y(zo).start()
+        self.x_to_c(zo).start()
+        self.to_y(zo).wait_recv()
+        if self.h1 is not None:
+            self.y_to_x(zo).start()
+        self.y_to_c(zo).start()
+
+    def on_far(self, zo):
+        self.x_to_y(zo).wait_recv()
+        self.far0_to_c(zo).start()
+        if self.h1 is not None:
+            self.y_to_x(zo).wait_recv()
+            self.far1_to_c(zo).start()
+
+    def start(self):
+        self.on_column(self.pos.z, True)
+
+    def round(self, r):
+        if 1 <= r < self.pos.depth:
+            self.pos.at(r, self.on_column)
+        if 1 <= r <= self.pos.depth:
+            self.pos.at(r - 1, self.on_sides)
+        if 2 <= r <= self.pos.depth + 1:
+            self.pos.at(r - 2, self.on_far)
+
+    def end_one(self, zo, mine=False):
+        split = self.h1 is not None
+        arrivals = [self.to_c(zo, mine), self.x_to_c(zo), self.y_to_c(zo), self.far0_to_c(zo)]
+        sends = [self.to_x(zo, mine), self.to_y(zo, mine), self.x_to_y(zo)] + arrivals
+        if split:
+            arrivals.append(self.far1_to_c(zo))
+            sends += [self.y_to_x(zo), self.far1_to_c(zo)]
+        for c in arrivals:
+            c.wait_recv()
+        self.along_z(zo, mine, lambda c: c.wait_send())
+        for c in sends:
+            c.wait_send()
+
+    def end(self):
+        self.end_one(self.pos.z, True)
+        for r in range(1, self.pos.depth):
+            self.pos.at(r, self.end_one)
+
+    @staticmethod
+    def sems(depth):
+        return [pltpu.SemaphoreType.DMA((Gather.SEND, depth)), pltpu.SemaphoreType.DMA((Gather.RECV, depth))]
+
+
+class Reduce:
+    SEND, RECV = 4 + 4 + 2, 4 + 4 + 2
+
+    def __init__(self, pos, part, core, far, side, column, send, recv):
+        self.pos, self.part = pos, part
+        self.core, self.far, self.side, self.column = core, far, side, column
+        self.send, self.recv = send, recv
+        rows = part.shape[1]
+        self.half = (pl.ds(0, rows // 2), pl.ds(rows // 2, rows // 2))
+        self.rounds = pos.depth + 2
+
+    @staticmethod
+    def scratch(depth, rows, width):
+        b = jnp.bfloat16
+        return [
+            pltpu.VMEM((depth, 4, rows, width), b),
+            pltpu.VMEM((depth, 2, rows // 2, width), b),
+            pltpu.VMEM((depth, 2, rows, width), b),
+            pltpu.VMEM((depth, 2, rows, width), b),
+            pltpu.SemaphoreType.DMA((Reduce.SEND, depth)),
+            pltpu.SemaphoreType.DMA((Reduce.RECV, depth)),
+        ]
+
+    def link(self, src, dst, k, zo, to):
+        return self.pos.copy(src, dst, self.send.at[k, zo], self.recv.at[k, zo], to)
+
+    def to_core(self, zo, fx, fy):
+        k = fx * 2 + fy
+        return self.link(self.part.at[self.pos.block(zo, fx, fy, 1)], self.core.at[zo, k], k, zo, "c")
+
+    def far_to(self, zo, k):
+        return self.link(self.core.at[zo, 3, self.half[k]], self.far.at[zo, k], 4 + k, zo, ("y", "x")[k])
+
+    def side_to(self, zo, k):
+        return self.link(self.core.at[zo, 2 - k], self.side.at[zo, k], 6 + k, zo, ("x", "y")[k])
+
+    def down(self, zo):
+        return self.link(self.core.at[zo, 0], self.column.at[zo, 0], 8, zo, "down")
+
+    def up(self, zo):
+        return self.link(self.core.at[zo, 0], self.column.at[zo, 1], 9, zo, "up")
+
+    def start_one(self, zo):
+        for fx, fy in ((1, 1), (1, 0), (0, 1), (0, 0)):
+            self.to_core(zo, fx, fy).start()
+
+    def start(self):
+        for dist in reversed(range(self.pos.depth)):
+            self.pos.at(dist, self.start_one)
+
+    def total(self, *refs):
+        f = refs[0][...].astype(jnp.float32)
+        for r in refs[1:]:
+            f = f + r[...].astype(jnp.float32)
+        return f
+
+    def on_core(self, zo):
+        for fx, fy in ((1, 1), (1, 0), (0, 1), (0, 0)):
+            k = fx * 2 + fy
+            self.to_core(zo, fx, fy).wait_recv()
+            mine = self.core.at[zo, k]
+            mine[...] = self.total(mine, self.part.at[self.pos.block(zo, fx, fy)]).astype(mine.dtype)
+            if k == 3:
+                self.far_to(zo, 0).start()
+                self.far_to(zo, 1).start()
+
+    def on_far(self, zo):
+        for k in range(2):
+            self.far_to(zo, k).wait_recv()
+            mine = self.core.at[zo, 2 - k, self.half[k]]
+            mine[...] = self.total(mine, self.far.at[zo, k]).astype(mine.dtype)
+            self.side_to(zo, k).start()
+
+    def on_sides(self, zo, mine=False):
+        z, depth = self.pos.z, self.pos.depth
+        self.side_to(zo, 0).wait_recv()
+        self.side_to(zo, 1).wait_recv()
+        here = self.core.at[zo, 0]
+        summed = self.total(here, self.side.at[zo, 0], self.side.at[zo, 1])
+        if mine:
+            self.out[...] = summed
+
+            @pl.when(z < depth - 1)
+            def _():
+                self.down(zo).wait_recv()
+                self.out[...] += self.column[zo, 0].astype(jnp.float32)
+
+            @pl.when(z > 0)
+            def _():
+                self.up(zo).wait_recv()
+                self.out[...] += self.column[zo, 1].astype(jnp.float32)
+
+            return
+        here[...] = summed.astype(here.dtype)
+
+        @pl.when((zo < z) & (z < depth - 1))
+        def _():
+            self.down(zo).wait_recv()
+            here[...] = self.total(here, self.column.at[zo, 0]).astype(here.dtype)
+
+        @pl.when((zo > z) & (z > 0))
+        def _():
+            self.up(zo).wait_recv()
+            here[...] = self.total(here, self.column.at[zo, 1]).astype(here.dtype)
+
+        @pl.when(zo < z)
+        def _():
+            self.down(zo).start()
+
+        @pl.when(zo > z)
+        def _():
+            self.up(zo).start()
+
+    def round(self, r):
+        depth = self.pos.depth
+        for s in range(3):
+            dist = depth - 1 - (r - s)
+            if not 0 <= dist < depth:
+                continue
+            if s == 0:
+                self.pos.at(dist, self.on_core)
+            elif s == 1:
+                self.pos.at(dist, self.on_far)
+            elif dist:
+                self.pos.at(dist, self.on_sides)
+            else:
+                self.on_sides(self.pos.z, True)
+
+    def end_one(self, zo):
+        for fx in range(2):
+            for fy in range(2):
+                self.to_core(zo, fx, fy).wait_send()
+        for k in range(2):
+            self.far_to(zo, k).wait_send()
+            self.side_to(zo, k).wait_send()
+
+        @pl.when(zo < self.pos.z)
+        def _():
+            self.down(zo).wait_send()
+
+        @pl.when(zo > self.pos.z)
+        def _():
+            self.up(zo).wait_send()
+
+    def end(self):
+        for r in range(self.pos.depth):
+            self.pos.at(r, self.end_one)
+
+
+def drive(*parts):
+    for p in parts:
+        p.start()
+    for r in range(max(p.rounds for p in parts)):
+        for p in parts:
+            p.round(r)
+    for p in parts:
+        p.end()
+
+
+def params(number, vmem=None):
+    return pltpu.CompilerParams(collective_id=number, has_side_effects=True, vmem_limit_bytes=vmem)
+
+
+def all_gather(depth, number, name, *blocks):
+    n = len(blocks)
+
+    def body(*refs):
+        own, out, sems, local = refs[:n], refs[n : 2 * n], refs[2 * n : 4 * n], refs[4 * n]
+        pos = Place(depth)
+        here = [pltpu.make_async_copy(own[i], out[i].at[pos.block(pos.z)], local.at[i]) for i in range(n)]
+        for c in here:
+            c.start()
+        pos.greet()
+        drive(*[Gather(pos, own[i], out[i], sems[2 * i], sems[2 * i + 1], own[i].shape[0] >= 32) for i in range(n)])
+        for c in here:
+            c.wait()
+
+    scratch = []
+    for _ in blocks:
+        scratch += Gather.sems(depth)
+    return pl.pallas_call(
+        body,
+        out_shape=[jax.ShapeDtypeStruct((depth * 8,) + b.shape, b.dtype) for b in blocks],
+        in_specs=[pl.BlockSpec(memory_space=HBM)] * n,
+        out_specs=[pl.BlockSpec(memory_space=HBM)] * n,
+        scratch_shapes=scratch + [pltpu.SemaphoreType.DMA((n,))],
+        compiler_params=params(number),
+        name=name,
+    )(*blocks)
+
+
+def reduce_scatter(depth, number, name, part, *blocks):
+    devices, rows, width = part.shape
+    n = len(blocks)
+
+    def body(part_ref, *refs):
+        own, out_sum, out = refs[:n], refs[n], refs[n + 1 : 2 * n + 1]
+        rest = refs[2 * n + 1 :]
+        pos = Place(depth)
+        here = [pltpu.make_async_copy(own[i], out[i].at[pos.block(pos.z)], rest[6].at[i]) for i in range(n)]
+        for c in here:
+            c.start()
+        pos.greet()
+        red = Reduce(pos, part_ref, *rest[:6])
+        red.out = out_sum
+        gathers = [
+            Gather(pos, own[i], out[i], rest[7 + 2 * i], rest[8 + 2 * i], own[i].shape[0] >= 32) for i in range(n)
+        ]
+        drive(red, *gathers)
+        for c in here:
+            c.wait()
+
+    scratch = Reduce.scratch(depth, rows, width) + [pltpu.SemaphoreType.DMA((max(n, 1),))]
+    for _ in blocks:
+        scratch += Gather.sems(depth)
+    return pl.pallas_call(
+        body,
+        out_shape=[jax.ShapeDtypeStruct((rows, width), jnp.float32)]
+        + [jax.ShapeDtypeStruct((devices,) + b.shape, b.dtype) for b in blocks],
+        in_specs=[pl.BlockSpec(memory_space=pltpu.VMEM)] + [pl.BlockSpec(memory_space=HBM)] * n,
+        out_specs=[pl.BlockSpec(memory_space=pltpu.VMEM)] + [pl.BlockSpec(memory_space=HBM)] * n,
+        scratch_shapes=scratch,
+        compiler_params=params(number, 40 * 2**20),
+        name=name,
+    )(part, *blocks)
+
+
+def exchange(groups, number, name, arrays, out_shapes, src_of, dst_of):
+    n = len(arrays)
+
+    def body(*refs):
+        src, out, send, recv, local = refs[:n], refs[n : 2 * n], refs[2 * n], refs[2 * n + 1], refs[2 * n + 2]
+        d = lax.axis_index("dp")
+        t = lax.axis_index("tensor")
+        here = [pltpu.make_async_copy(src_of(i, src[i], d), dst_of(i, out[i], d), local.at[i]) for i in range(n)]
+        for c in here:
+            c.start()
+        barrier = pltpu.get_barrier_semaphore()
+        peers = [lax.rem(d + p, groups) for p in range(1, groups)]
+        for p in peers:
+            pl.semaphore_signal(barrier, inc=1, device_id=(p, t), device_id_type=MESH)
+        pl.semaphore_wait(barrier, groups - 1)
+        copies = []
+        for k, p in enumerate(peers):
+            for i in range(n):
+                copies.append(
+                    pltpu.make_async_remote_copy(
+                        src_ref=src_of(i, src[i], p),
+                        dst_ref=dst_of(i, out[i], d),
+                        send_sem=send.at[i, k],
+                        recv_sem=recv.at[i, k],
+                        device_id=(p, t),
+                        device_id_type=MESH,
+                    )
+                )
+                copies[-1].start()
+        for c in copies:
+            c.wait()
+        for c in here:
+            c.wait()
+
+    return pl.pallas_call(
+        body,
+        out_shape=out_shapes,
+        in_specs=[pl.BlockSpec(memory_space=HBM)] * n,
+        out_specs=[pl.BlockSpec(memory_space=HBM)] * n,
+        scratch_shapes=[
+            pltpu.SemaphoreType.DMA((n, groups - 1)),
+            pltpu.SemaphoreType.DMA((n, groups - 1)),
+            pltpu.SemaphoreType.DMA((n,)),
+        ],
+        compiler_params=params(number),
+        name=name,
+    )(*arrays)
+
+
+def head_shards(
+    tokens,
+    segments,
+    routes,
+    out_grad,
+    norm_gain,
+    q_weight,
+    k_weight,
+    v_weight,
+    q_gain,
+    k_gain,
+    out_weight,
+    moe_gain,
+    router_weight,
+    gate_weight,
+    up_weight,
+    down_weight,
+):
+    f32, bf = jnp.float32, jnp.bfloat16
+    head_dim = q_gain.shape[0]
+    tok_rows, width = tokens.shape
+    share_rows = out_grad.shape[0]
+    all_tokens = segments.shape[0]
+    expert_count = router_weight.shape[1]
+    top_count = routes.shape[1]
+    groups = all_tokens // tok_rows
+    depth = groups // 2
+    weight_rows = q_weight.shape[0]
+    capacity = max(2, share_rows * top_count * 2 // expert_count)
+    slots = capacity * expert_count
+    score_scale = head_dim ** (-0.5)
+    lane = lax.axis_index("tensor")
+    expert = lax.axis_index("dp") * 4 + lane
+
+    places = jnp.arange(all_tokens, dtype=jnp.int32)
+    begins = jnp.concatenate([jnp.ones((1,), dtype=bool), segments[1:] != segments[:-1]])
+    positions = places - lax.cummax(jnp.where(begins, places, 0), axis=0)
+    cosine, sine_part = angles(positions, head_dim)
+    allowed = (places[None, :] <= places[:, None]) & (segments[None, :] == segments[:, None])
+
+    tokens_share = lax.dynamic_slice_in_dim(tokens, lane * share_rows, share_rows, 0)
+    routes_block = jnp.zeros((8, 128), jnp.int32).at[: share_rows * top_count // 128].set(routes.reshape(-1, 128))
+    all_tok, all_routes = all_gather(depth, 0, "gather_tokens", tokens_share, routes_block)
+    all_tok = all_tok.reshape(all_tokens, width)
+    all_routes = all_routes[:, : share_rows * top_count // 128].reshape(all_tokens, top_count)
+
+    def rows_of(ref, p):
+        return ref.at[pl.ds(p * weight_rows, weight_rows)]
+
+    def cols_of(ref, p):
+        return ref.at[:, pl.ds(pl.multiple_of(p * head_dim, head_dim), head_dim)]
+
+    head_weight = jax.ShapeDtypeStruct((width, head_dim), bf)
+    w_q, w_o, w_k, w_v = exchange(
+        groups,
+        1,
+        "exchange_weights",
+        [q_weight, out_weight, k_weight, v_weight],
+        [head_weight] * 4,
+        lambda i, ref, p: cols_of(ref, p) if i < 2 else ref,
+        lambda i, ref, p: rows_of(ref, p),
+    )
+    (all_grad,) = all_gather(depth, 2, "gather_out_grad", out_grad)
+    all_grad = all_grad.reshape(all_tokens, width)
+
+    tok_float = all_tok.astype(f32)
+    norm_gain_float = norm_gain.astype(f32)
+    hidden = norm_rows(tok_float, norm_gain_float).astype(bf)
+    w_in = jnp.concatenate([w_q, w_k, w_v], axis=1)
+    projected = jnp.dot(hidden, w_in, preferred_element_type=f32)
+
+    def prepare_local(projected_in, qgain_in, kgain_in):
+        return prepare(projected_in, qgain_in, kgain_in, cosine, sine_part, head_dim)
+
+    prepared, prepare_back = jax.vjp(prepare_local, projected, q_gain.astype(f32), k_gain.astype(f32))
+    queries = prepared[0].astype(bf).reshape(all_tokens, head_dim)
+    keys = prepared[1].astype(bf)
+    values = prepared[2].astype(bf)
+    scores = jnp.einsum("td,nd->tn", queries, keys, preferred_element_type=f32) * score_scale
+    scores = jnp.where(allowed, scores, -1e30)
+    top = jnp.max(scores, axis=-1, keepdims=True)
+    weights = jnp.exp(scores - top)
+    mass = jnp.sum(weights, axis=-1, keepdims=True)
+    log_total = top + jnp.log(mass)
+    head_out = jnp.dot(weights.astype(bf), values, preferred_element_type=f32) / mass
+    attended = head_out.astype(bf)
+    branch_part = jnp.einsum("tc,dc->td", attended, w_o, preferred_element_type=f32).astype(bf)
+    (branch,) = reduce_scatter(
+        depth, 3, "reduce_branch", branch_part.reshape(expert_count, share_rows, width)
+    )
+
+    middle = tokens_share.astype(f32) + branch
+    normed_float, moe_norm_back = jax.vjp(norm_rows, middle, moe_gain.astype(f32))
+    (normed,) = all_gather(depth, 4, "gather_normed", normed_float.astype(bf))
+    normed = normed.reshape(all_tokens, width)
+    logits = jnp.dot(normed, router_weight, preferred_element_type=f32)
+    named = jnp.any(all_routes[:, :, None] == jnp.arange(expert_count, dtype=jnp.int32), axis=1)
+
+    probabilities = jax.nn.softmax(logits, axis=-1)
+    chosen = jnp.where(named, probabilities, 0.0)
+    gate_all = chosen / jnp.sum(chosen, axis=1, keepdims=True)
+    here = jnp.arange(expert_count, dtype=jnp.int32) == expert
+    mine = jnp.any(named & here, axis=1)
+    gate_mine = jnp.sum(jnp.where(here, gate_all, 0.0), axis=1)
+    rank = jnp.cumsum(mine.astype(jnp.int32)) - 1
+    select = ((rank[None, :] == jnp.arange(slots, dtype=jnp.int32)[:, None]) & mine[None, :]).astype(bf)
+    inputs = jnp.dot(select, normed, preferred_element_type=f32).astype(bf)
+    grads = jnp.dot(select, all_grad, preferred_element_type=f32)
+    gate_rows = jnp.sum(jnp.where(select > 0, gate_mine[None, :], 0.0), axis=1)
+    w_gate, w_up, w_down = gate_weight[0], up_weight[0], down_weight[0]
+    gate_act = jnp.dot(inputs, w_gate, preferred_element_type=f32)
+    up_act = jnp.dot(inputs, w_up, preferred_element_type=f32)
+    inner_float, swiglu_back = jax.vjp(swiglu, gate_act, up_act)
+    inner_act = inner_float.astype(bf)
+    returned = jnp.dot(inner_act, w_down, preferred_element_type=f32).astype(bf)
+    grad_returned = (gate_rows[:, None] * grads).astype(bf)
+    grad_gate_rows = jnp.sum(grads * returned.astype(f32), axis=1)
+    out_rows = (gate_rows[:, None] * returned.astype(f32)).astype(bf)
+    out_part = jnp.einsum("rt,rd->td", select, out_rows, preferred_element_type=f32).astype(bf)
+    (out_sum,) = reduce_scatter(
+        depth, 5, "reduce_out", out_part.reshape(expert_count, share_rows, width)
+    )
+    layer_out = (middle + out_sum).astype(bf)
+    grad_inner = jnp.einsum("rd,fd->rf", grad_returned, w_down, preferred_element_type=f32)
+    grad_down = jnp.einsum("rf,rd->fd", inner_act, grad_returned, preferred_element_type=f32)
+    grad_gate_float, grad_up_float = swiglu_back(grad_inner)
+    grad_gate_act = grad_gate_float.astype(bf)
+    grad_up_act = grad_up_float.astype(bf)
+    grad_gate_w = jnp.einsum("rd,rf->df", inputs, grad_gate_act, preferred_element_type=f32)
+    grad_up_w = jnp.einsum("rd,rf->df", inputs, grad_up_act, preferred_element_type=f32)
+    grad_inputs = jnp.einsum("rf,df->rd", grad_gate_act, w_gate, preferred_element_type=f32)
+    grad_inputs = (
+        grad_inputs + jnp.einsum("rf,df->rd", grad_up_act, w_up, preferred_element_type=f32)
+    ).astype(bf)
+    grad_gate_mine = jnp.sum(jnp.where(select > 0, grad_gate_rows[:, None], 0.0), axis=0)
+    own_grad = jnp.where(here, grad_gate_mine[:, None], 0.0)
+    own_logit_grad = gate_all * (own_grad - jnp.sum(gate_all * own_grad, axis=1, keepdims=True))
+    normed_part = jnp.einsum("rt,rd->td", select, grad_inputs, preferred_element_type=f32) + jnp.einsum(
+        "te,de->td", own_logit_grad.astype(bf), router_weight, preferred_element_type=f32
+    )
+    (grad_normed,) = reduce_scatter(
+        depth, 6, "reduce_normed", normed_part.astype(bf).reshape(expert_count, share_rows, width)
+    )
+    grad_middle_part, grad_moe_gain = moe_norm_back(grad_normed)
+    grad_middle = out_grad.astype(f32) + grad_middle_part
+    all_branch, all_gate_grads = all_gather(
+        depth, 7, "gather_grad_branch", grad_middle.astype(bf), grad_gate_mine.reshape(8, -1)
+    )
+    grad_branch = all_branch.reshape(all_tokens, width)
+    gate_grads = all_gate_grads.reshape(expert_count, all_tokens).T
+    logit_grads = gate_all * (gate_grads - jnp.sum(gate_all * gate_grads, axis=1, keepdims=True))
+    grad_router = jnp.einsum("td,te->de", normed, logit_grads.astype(bf), preferred_element_type=f32)
+
+    grad_heads = jnp.dot(grad_branch, w_o, preferred_element_type=f32).astype(bf)
+    out_weight_part = jnp.einsum("td,tc->dc", grad_branch, attended, preferred_element_type=f32).astype(bf)
+    row_delta = jnp.sum(grad_heads.astype(f32) * head_out, axis=-1, keepdims=True)
+    scores = jnp.einsum("td,nd->tn", queries, keys, preferred_element_type=f32) * score_scale
+    soft = jnp.where(allowed, jnp.exp(scores - log_total), 0.0)
+    grad_soft = jnp.einsum("td,nd->tn", grad_heads, values, preferred_element_type=f32)
+    grad_scores = (soft * (grad_soft - row_delta)).astype(bf)
+    grad_queries = jnp.dot(grad_scores, keys, preferred_element_type=f32) * score_scale
+    grad_keys = jnp.einsum("tn,td->nd", grad_scores, queries, preferred_element_type=f32) * score_scale
+    grad_values = jnp.einsum("tn,td->nd", soft.astype(bf), grad_heads, preferred_element_type=f32)
+    grad_proj_float, grad_q_gain, grad_k_gain = prepare_back((grad_queries[:, None, :], grad_keys, grad_values))
+    grad_projected = grad_proj_float.astype(bf)
+    hidden_part = jnp.einsum("tc,dc->td", grad_projected, w_in, preferred_element_type=f32)
+    _, first_norm_back = jax.vjp(norm_rows, tok_float, norm_gain_float)
+    in_weight_part = jnp.einsum("td,tc->dc", hidden, grad_projected, preferred_element_type=f32).astype(bf)
+    normalised = norm_rows(tok_float, 1.0)
+    grad_norm_gain = jnp.sum(hidden_part * normalised, axis=0)
+    small = jnp.concatenate([grad_norm_gain, grad_moe_gain, grad_q_gain, grad_k_gain])
+    small_rows = -(-small.shape[0] // 1024) * 8
+    small_block = jnp.pad(small, (0, small_rows * 128 - small.shape[0])).reshape(small_rows, 128)
+    grad_hidden, all_small = reduce_scatter(
+        depth, 8, "reduce_hidden", hidden_part.astype(bf).reshape(expert_count, share_rows, width), small_block
+    )
+    _, share_norm_back = jax.vjp(norm_rows, tokens_share.astype(f32), norm_gain_float)
+    tokens_grad = grad_middle + share_norm_back(grad_hidden)[0]
+    small_sums = jnp.sum(all_small, axis=0).reshape(-1)
+    grad_q, grad_o, grad_kv = exchange(
+        groups,
+        9,
+        "exchange_weight_grads",
+        [in_weight_part[:, :head_dim], out_weight_part, in_weight_part[:, head_dim:]],
+        [jax.ShapeDtypeStruct(q_weight.shape, bf)] * 2
+        + [jax.ShapeDtypeStruct((groups, weight_rows, 2 * head_dim), bf)],
+        lambda i, ref, p: rows_of(ref, p),
+        lambda i, ref, p: cols_of(ref, p) if i < 2 else ref.at[p],
+    )
+    kv_sum = jnp.sum(grad_kv.astype(f32), axis=0)
+    return (
+        layer_out,
+        tokens_grad,
+        small_sums[:width],
+        grad_q.astype(f32),
+        kv_sum[:, :head_dim],
+        kv_sum[:, head_dim:],
+        small_sums[2 * width : 2 * width + head_dim],
+        small_sums[2 * width + head_dim : 2 * width + 2 * head_dim],
+        grad_o.astype(f32),
+        small_sums[width : 2 * width],
+        grad_router,
+        grad_gate_w[None],
+        grad_up_w[None],
+        grad_down[None],
+    )
+
+
 def solution(mesh):
+    per_device = shards if mesh.shape["dp"] != 8 or mesh.shape["tensor"] != 4 else head_shards
     placed = (
         P("dp", None),
         P(),
@@ -367,7 +1061,7 @@
         P(("dp", "tensor"), None, None),
     )
     return jax.shard_map(
-        shards,
+        per_device,
         mesh=mesh,
         in_specs=placed,
         out_specs=(

time: 915 us -> 461 us (0.50)
  the two profiles are of different devices: /device:TPU:0 before, /device:TPU:11 now
where the time goes in v1:
time: 461 us; the launch traced here: 453 us
  Pallas kernels  310 us (67%)
  matrix products  84.6 us (18%)
  other arithmetic  33.2 us (7%)
  local copies, waits for them, and re-layouts  23.9 us (5%)
    pallas_call x4, Pallas kernels, all_gather(): pl.pallas_call(body, out_shape=[jax.ShapeDtypeStruct((depth * 8,) + b.sha...  106 us
    pallas_call x2, Pallas kernels, exchange(): pl.pallas_call(body, out_shape=out_shapes, in_specs=[pl.BlockSpec(memory_...  103 us
    pallas_call x4, Pallas kernels, reduce_scatter(): pl.pallas_call(body, out_shape=[jax.ShapeDtypeStruct((rows, width), jnp.f...  101 us
    unnamed x151, local copies, waits for them, and re-layouts  10.1 us
    dot_general x1, matrix products, head_shards(): jnp.einsum('rt,rd->td', select, grad_inputs, preferred_element_type=f32)  9.69 us

profile of v1, /device:TPU:11, one launch (start us, length us, event | category | flops | bytes accessed | tf_op | source)
XLA Modules:
  0.0 453.5 jit_solution(9711671358924871287)
XLA Ops:
  0.7 0.8 convert_element_type.162
  1.5 0.7 convert_element_type.165
  2.3 0.8 slice_compare_fusion
  5.2 0.8 copy.36
  6.6 1.6 constant_dynamic-slice_fusion.refs_0_
  8.2 50.5 %exchange_weights.1 = (bf16[2048,128]{1,0:T(8,128)(2,1)}, bf16[2048,128]{1,0:T(8,128)(2,1)}, bf16[2048,128]{1,0:T(8,128)(2,1)}, bf16[2048,128]{1,0:T(8,128)(2,1)}) custom-call(bf16[256,1024]{1,0:T(8,128)(2,1)} %refs_0_.2, bf16[256,1024]{1,0:T(8,128)(2,1)} %refs_1_.1, bf16[256,128]{1,0:T(8,128)(2,1)} %refs_2_.1, bf16[256,128]{1,0:T(8,128)(2,1)} %refs_3_.1), custom_call_target="tpu_custom_call" | custom-call | tf_op jit(solution)/shard_map/exchange_weights/pallas_call | solution.py:820
  58.7 2.0 constant_dynamic-update-slice_fusion.2
  60.6 2.0 constant_dynamic-update-slice_fusion.1
  62.7 1.9 constant_dynamic-update-slice_fusion
  64.6 26.8 %gather_tokens.1 = (bf16[32,32,2048]{2,1,0:T(8,128)(2,1)}, s32[32,8,128]{2,1,0:T(8,128)}) custom-call(bf16[32,2048]{1,0:T(8,128)(2,1)} %constant_dynamic-slice_fusion.refs_0_, s32[8,128]{1,0:T(8,128)} %scatter.4.refs_1_), custom_call_target="tpu_custom_call" | custom-call | tf_op jit(solution)/shard_map/gather_tokens/pallas_call | solution.py:739
  91.4 0.9 slice.108
  92.4 3.1 multiply_reduce_fusion.1
  95.5 1.1 eq.54
  96.6 1.2 copy.37
  100.4 3.2 multiply_convert_fusion
  103.6 4.5 fusion.133
  109.5 1.2 fusion.105
  110.7 2.5 fusion.84
  113.2 25.3 %gather_out_grad.1 = bf16[32,32,2048]{2,1,0:T(8,128)(2,1)} custom-call(bf16[32,2048]{1,0:T(8,128)(2,1)} %refs_0_.3), custom_call_target="tpu_custom_call" | custom-call | tf_op jit(solution)/shard_map/gather_out_grad/pallas_call | solution.py:739
  138.6 1.9 fusion.130
  140.5 1.7 fusion.3
  142.8 2.2 fusion.42
  145.1 1.3 convolution_convert_fusion.1
  146.4 24.0 %reduce_branch.1 = f32[32,2048]{1,0:T(8,128)S(1)} custom-call(bf16[32,32,2048]{2,1,0:T(8,128)(2,1)S(1)} %bitcast.142), custom_call_target="tpu_custom_call" | custom-call | tf_op jit(solution)/shard_map/reduce_branch/pallas_call | solution.py:774
  170.4 1.1 multiply_reduce_fusion.9
  172.7 0.7 multiply_convert_fusion.5.refs_0_
  173.4 27.7 %gather_normed.1 = bf16[32,32,2048]{2,1,0:T(8,128)(2,1)} custom-call(bf16[32,2048]{1,0:T(8,128)(2,1)} %multiply_convert_fusion.5.refs_0_), custom_call_target="tpu_custom_call" | custom-call | tf_op jit(solution)/shard_map/gather_normed/pallas_call | solution.py:739
  201.1 3.7 fusion.132
  205.0 2.4 convolution_convert_fusion.2
  207.4 1.8 fusion.15
  209.2 0.8 copy-done.69
  210.0 1.9 multiply_convert_fusion.4
  212.0 1.8 fusion.17
  214.2 2.5 fusion.1
  218.6 3.3 fusion.40
  221.9 4.6 %convolution_bitcast_fusion = f32[1,768,2048]{2,1,0:T(8,128)} fusion(bf16[512,768]{1,0:T(8,128)(2,1)S(1)} %get-tuple-element.93, f32[512,2048]{1,0:T(8,128)S(1)} %get-tuple-element.96, f32[512]{0:T(512)S(1)} %select_reduce_fusion.1), kind=kOutput, calls=%fused_computation.18 | convolution fusion | flops 1612709888 | bytes 11274240 | tf_op jit(solution)/shard_map/rf,rd->fd/dot_general | solution.py:959
  226.6 2.5 convolution_convert_fusion
  229.0 23.5 %reduce_out.1 = f32[32,2048]{1,0:T(8,128)S(1)} custom-call(bf16[32,32,2048]{2,1,0:T(8,128)(2,1)S(1)} %bitcast.145), custom_call_target="tpu_custom_call" | custom-call | tf_op jit(solution)/shard_map/reduce_out/pallas_call | solution.py:774
  252.6 3.8 fusion.9
  256.4 9.7 %fusion.29 = f32[1024,2048]{1,0:T(8,128)} fusion(s32[1024]{0:T(1024)} %add_bitcast_fusion, pred[1024]{0:T(1024)(128)(4,1)} %copy-done.61, f32[512,2048]{1,0:T(8,128)} %fusion.9, bf16[512,768]{1,0:T(8,128)(2,1)} %get-tuple-element.69, bf16[1,2048,768]{2,1,0:T(8,128)(2,1)S(1)} %copy-done), kind=kOutput, calls=%fused_computation.50 | convolution fusion | flops 3761242112 | bytes 16520192 | tf_op jit(solution)/shard_map/rt,rd->td/dot_general | solution.py:972
  266.1 4.8 %add_convert_fusion = bf16[1024,2048]{1,0:T(8,128)(2,1)S(1)} fusion(f32[1024,2048]{1,0:T(8,128)} %fusion.29, bf16[2048,32]{0,1:T(8,128)(2,1)} %param.30, f32[1024,32]{0,1:T(8,128)S(1)} %get-tuple-element.64, f32[1024]{0:T(1024)} %get-tuple-element.60, f32[1024]{0:T(1024)} %copy-done.41, pred[32]{0:T(512)(128)(4,1)} %copy-done.54), kind=kOutput, calls=%fused_computation.2 | convolution fusion | flops 138543104 | bytes 12853280 | tf_op jit(solution)/shard_map/te,de->td/dot_general | solution.py:972
  271.0 27.3 %reduce_normed.1 = f32[32,2048]{1,0:T(8,128)S(1)} custom-call(bf16[32,32,2048]{2,1,0:T(8,128)(2,1)S(1)} %bitcast.143), custom_call_target="tpu_custom_call" | custom-call | tf_op jit(solution)/shard_map/reduce_normed/pallas_call | solution.py:774
  299.1 0.8 fusion.129.refs_0_
  299.8 26.4 %gather_grad_branch.1 = (bf16[32,32,2048]{2,1,0:T(8,128)(2,1)}, f32[32,8,128]{2,1,0:T(8,128)}) custom-call(bf16[32,2048]{1,0:T(8,128)(2,1)} %fusion.129.refs_0_, f32[8,128]{1,0:T(8,128)} %bitcast.154), custom_call_target="tpu_custom_call" | custom-call | tf_op jit(solution)/shard_map/gather_grad_branch/pallas_call | solution.py:739
  326.3 3.9 multiply_reduce_fusion.4
  330.2 2.1 convolution_convert_fusion.4.refs_1_
  332.4 1.5 fusion.107
  333.9 0.9 fusion.36
  335.4 2.6 multiply_convert_fusion.1
  338.6 0.8 convolution_multiply_fusion.1
  339.4 1.2 fusion.87
  340.6 1.2 fusion.81
  342.5 3.6 convolution_convert_fusion.3
  346.1 4.9 %multiply_reduce_fusion = (f32[2048]{0:T(1024)S(1)}, bf16[1024,2048]{1,0:T(8,128)(2,1)S(1)}) fusion(bf16[32,32,2048]{2,1,0:T(8,128)(2,1)S(1)} %copy-done.5, f32[1024]{0:T(1024)S(1)} %copy-done.48, bf16[2048,384]{1,0:T(8,128)(2,1)} %constant_dynamic-update-slice_fusion, f32[1024,128]{0,1:T(8,128)S(1)} %fusion.58, f32[1024,128]{0,1:T(8,128)S(1)} %add_add_fusion.1, ...), kind=kOutput, calls=%fused_computation.1 | convolution fusion | flops 1622276096 | bytes 11546624 | tf_op jit(solution)/shard_map/tc,dc->td/dot_general | solution.py:1000
  351.1 25.8 %reduce_hidden.1 = (f32[32,2048]{1,0:T(8,128)S(1)}, f32[32,40,128]{2,1,0:T(8,128)S(1)}) custom-call(bf16[32,32,2048]{2,1,0:T(8,128)(2,1)S(1)} %bitcast.144, f32[40,128]{1,0:T(8,128)S(1)} %fusion.115.refs_0_), custom_call_target="tpu_custom_call" | custom-call | tf_op jit(solution)/shard_map/reduce_hidden/pallas_call | solution.py:774
  378.3 0.9 fusion.90
  379.2 1.9 slice.133.refs_0_
  381.1 2.3 slice.134.refs_2_
  383.3 52.5 %exchange_weight_grads.1 = (bf16[256,1024]{1,0:T(8,128)(2,1)}, bf16[256,1024]{1,0:T(8,128)(2,1)}, bf16[8,256,256]{2,1,0:T(8,128)(2,1)}) custom-call(bf16[2048,128]{1,0:T(8,128)(2,1)} %slice.133.refs_0_, bf16[2048,128]{1,0:T(8,128)(2,1)} %convolution_convert_fusion.4.refs_1_, bf16[2048,256]{1,0:T(8,128)(2,1)} %slice.134.refs_2_), custom_call_target="tpu_custom_call" | custom-call | tf_op jit(solution)/shard_map/exchange_weight_grads/pallas_call | solution.py:820
  435.9 1.4 convert_reduce_fusion
  438.0 2.1 convert_element_type.197
  440.1 2.1 convert_element_type.199
  442.3 6.5 %convolution_bitcast_fusion.2 = f32[1,2048,768]{2,1,0:T(8,128)} fusion(bf16[512,2048]{1,0:T(8,128)(2,1)} %copy-done.70, bf16[512,768]{1,0:T(8,128)(2,1)} %get-tuple-element.69), kind=kOutput, calls=%fused_computation.20 | convolution fusion | flops 1610612736 | bytes 9175040 | tf_op jit(solution)/shard_map/rd,rf->df/dot_general | solution.py:963
  448.7 4.6 %convolution_bitcast_fusion.1 = f32[1,2048,768]{2,1,0:T(8,128)} fusion(bf16[512,2048]{1,0:T(8,128)(2,1)S(1)} %copy-done.71, bf16[512,768]{1,0:T(8,128)(2,1)S(1)} %copy-done.73), kind=kOutput, calls=%fused_computation.19 | convolution fusion | flops 1610612736 | bytes 9175040 | tf_op jit(solution)/shard_map/rd,rf->df/dot_general | solution.py:964
  (196 shorter events, 15.6 us)
Async XLA Ops:
  0.6 206.7 %copy-start = (bf16[1,2048,768]{2,1,0:T(8,128)(2,1)S(1)}, bf16[1,2048,768]{2,1,0:T(8,128)(2,1)}, u32[]{:S(2)}) copy-start(bf16[1,2048,768]{2,1,0:T(8,128)(2,1)} %param.31) | copy-start | bytes 9437188
  0.7 97.3 %copy-start.54 = (pred[32]{0:T(512)(128)(4,1)}, pred[32]{0:T(512)(128)(4,1)S(1)}, u32[]{:S(2)}) copy-start(pred[32]{0:T(512)(128)(4,1)S(1)} %iota_compare_fusion.4) | copy-start | bytes 100
  0.7 108.7 %copy-start.52 = (f32[64]{0:T(128)}, f32[64]{0:T(128)S(1)}, u32[]{:S(2)}) copy-start(f32[64]{0:T(128)S(1)} %multiply_power_fusion) | copy-start | bytes 772
  1.5 107.4 %copy-start.56 = (f32[128]{0:T(128)}, f32[128]{0:T(128)S(1)}, u32[]{:S(2)}) copy-start(f32[128]{0:T(128)S(1)} %convert_element_type.162) | copy-start | bytes 1540
  2.3 106.6 %copy-start.58 = (f32[128]{0:T(128)}, f32[128]{0:T(128)S(1)}, u32[]{:S(2)}) copy-start(f32[128]{0:T(128)S(1)} %convert_element_type.165) | copy-start | bytes 1540
  3.8 105.7 %copy-start.33 = (f32[1024]{0:T(1024)}, f32[1024]{0:T(1024)S(1)}, u32[]{:S(2)}) copy-start(f32[1024]{0:T(1024)S(1)} %fusion.117) | copy-start | bytes 12292
  95.5 8.1 %copy-start.47 = (f32[1024]{0:T(1024)}, f32[1024]{0:T(1024)S(1)}, u32[]{:S(2)}) copy-start(f32[1024]{0:T(1024)S(1)} %rsqrt.54) | copy-start | bytes 12292
  103.6 4.5 copy-start.12
  108.2 2.4 copy-start.44
  108.9 1.8 copy-start.35
  109.2 1.4 copy-start.37
  110.6 29.8 %copy-start.24 = (bf16[1024,64]{0,1:T(8,128)(2,1)}, bf16[1024,64]{0,1:T(8,128)(2,1)S(1)}, u32[]{:S(2)}) copy-start(bf16[1024,64]{0,1:T(8,128)(2,1)S(1)} %get-tuple-element.77) | copy-start | bytes 393220
  110.6 29.8 %copy-start.26 = (bf16[1024,64]{0,1:T(8,128)(2,1)}, bf16[1024,64]{0,1:T(8,128)(2,1)S(1)}, u32[]{:S(2)}) copy-start(bf16[1024,64]{0,1:T(8,128)(2,1)S(1)} %get-tuple-element.78) | copy-start | bytes 393220
  113.2 27.3 %copy-start.28 = (bf16[1024,64]{0,1:T(8,128)(2,1)}, bf16[1024,64]{0,1:T(8,128)(2,1)S(1)}, u32[]{:S(2)}) copy-start(bf16[1024,64]{0,1:T(8,128)(2,1)S(1)} %get-tuple-element.79) | copy-start | bytes 393220
  138.5 2.0 copy-start.39
  140.5 2.3 copy-start.14
  142.8 2.2 copy-start.17
  146.3 54.8 %copy-start.21 = (bf16[2048,32]{0,1:T(8,128)(2,1)S(1)}, bf16[2048,32]{0,1:T(8,128)(2,1)}, u32[]{:S(2)}) copy-start(bf16[2048,32]{0,1:T(8,128)(2,1)} %param.30) | copy-start | bytes 393220
  173.4 31.4 %copy-start.32 = (pred[1024,32]{0,1:T(8,128)(4,1)S(1)}, pred[1024,32]{0,1:T(8,128)(4,1)}, u32[]{:S(2)}) copy-start(pred[1024,32]{0,1:T(8,128)(4,1)} %copy-done.31) | copy-start | bytes 98308
  173.4 31.5 %copy-start.62 = (pred[1024]{0:T(1024)(128)(4,1)S(1)}, pred[1024]{0:T(1024)(128)(4,1)}, u32[]{:S(2)}) copy-start(pred[1024]{0:T(1024)(128)(4,1)} %copy-done.61) | copy-start | bytes 3076
  173.4 31.5 %copy-start.63 = (s32[1024]{0:T(1024)S(1)}, s32[1024]{0:T(1024)}, u32[]{:S(2)}) copy-start(s32[1024]{0:T(1024)} %add_bitcast_fusion) | copy-start | bytes 12292
  201.1 3.9 copy-start.2
  207.4 1.8 copy-start.70
  207.4 2.6 copy-start.69
  210.0 1.9 copy-start.68
  212.0 2.2 copy-start.16
  214.2 3.0 copy-start.55
  217.2 4.7 %copy-start.41 = (f32[1024]{0:T(1024)}, f32[1024]{0:T(1024)S(1)}, u32[]{:S(2)}) copy-start(f32[1024]{0:T(1024)S(1)} %select_reduce_fusion) | copy-start | bytes 12292
  221.9 30.6 %copy-start.72 = (bf16[512,768]{1,0:T(8,128)(2,1)}, bf16[512,768]{1,0:T(8,128)(2,1)S(1)}, u32[]{:S(2)}) copy-start(bf16[512,768]{1,0:T(8,128)(2,1)S(1)} %get-tuple-element.70) | copy-start | bytes 2359300
  270.9 27.3 %copy-start.11 = (f32[32,2048]{1,0:T(8,128)S(1)}, f32[32,2048]{1,0:T(8,128)}, u32[]{:S(2)}) copy-start(f32[32,2048]{1,0:T(8,128)} %copy-done.10) | copy-start | bytes 786436
  270.9 27.3 %copy-start.50 = (f32[32]{0:T(128)S(1)}, f32[32]{0:T(128)}, u32[]{:S(2)}) copy-start(f32[32]{0:T(128)} %copy-done.49) | copy-start | bytes 388
  270.9 28.1 %copy-start.67 = (f32[32]{0:T(128)S(1)}, f32[32]{0:T(128)}, u32[]{:S(2)}) copy-start(f32[32]{0:T(128)} %copy-done.66) | copy-start | bytes 388
  271.0 28.1 %copy-start.19 = (bf16[32,2048]{1,0:T(8,128)(2,1)S(1)}, bf16[32,2048]{1,0:T(8,128)(2,1)}, u32[]{:S(2)}) copy-start(bf16[32,2048]{1,0:T(8,128)(2,1)} %refs_0_.3) | copy-start | bytes 393220
  271.0 55.3 %copy-start.9 = (f32[1024,128]{0,1:T(8,128)S(1)}, f32[1024,128]{0,1:T(8,128)}, u32[]{:S(2)}) copy-start(f32[1024,128]{0,1:T(8,128)} %copy-done.8) | copy-start | bytes 1572868
  271.0 55.3 %copy-start.18 = (bf16[2048,128]{1,0:T(8,128)(2,1)S(1)}, bf16[2048,128]{1,0:T(8,128)(2,1)}, u32[]{:S(2)}) copy-start(bf16[2048,128]{1,0:T(8,128)(2,1)} %get-tuple-element.43) | copy-start | bytes 1572868
  299.1 31.1 %copy-start.64 = (f32[32]{0:T(128)}, f32[32]{0:T(128)S(1)}, u32[]{:S(2)}) copy-start(f32[32]{0:T(128)S(1)} %multiply_multiply_fusion.4) | copy-start | bytes 388
  326.2 3.9 copy-start.4
  326.3 6.1 %copy-start.23 = (f32[32,8,128]{2,1,0:T(8,128)S(1)}, f32[32,8,128]{2,1,0:T(8,128)}, u32[]{:S(2)}) copy-start(f32[32,8,128]{2,1,0:T(8,128)} %get-tuple-element.51) | copy-start | bytes 393220
  330.2 2.2 copy-start.3
  330.2 3.8 copy-start.15
  330.2 3.8 copy-start.40
  330.2 3.7 copy-start.60
  333.9 1.4 copy-start.7
  335.3 2.6 copy-start.29
  335.4 2.7 copy-start.30
  335.4 3.2 copy-start.25
  335.4 3.2 copy-start.27
  338.0 3.8 copy-start.38
  338.0 3.8 copy-start.59
  338.1 3.9 copy-start.36
  338.1 3.9 copy-start.57
  338.6 3.6 copy-start.43
  338.6 3.6 copy-start.45
  339.4 3.0 copy-start.13
  342.5 3.6 copy-start.5
  342.5 3.6 copy-start.48
  346.1 4.9 %copy-start.46 = (f32[2048]{0:T(1024)S(1)}, f32[2048]{0:T(1024)}, u32[]{:S(2)}) copy-start(f32[2048]{0:T(1024)} %get-tuple-element.58) | copy-start | bytes 24580
  351.0 27.0 %copy-start.22 = (bf16[128,2048]{1,0:T(8,128)(2,1)S(1)}, bf16[128,2048]{1,0:T(8,128)(2,1)}, u32[]{:S(2)}) copy-start(bf16[128,2048]{1,0:T(8,128)(2,1)} %param.18) | copy-start | bytes 1572868
  351.0 27.2 %copy-start.20 = (bf16[32,2048]{1,0:T(8,128)(2,1)S(1)}, bf16[32,2048]{1,0:T(8,128)(2,1)}, u32[]{:S(2)}) copy-start(bf16[32,2048]{1,0:T(8,128)(2,1)} %refs_0_.3) | copy-start | bytes 393220
  351.1 27.2 %copy-start.51 = (f32[32]{0:T(128)S(1)}, f32[32]{0:T(128)}, u32[]{:S(2)}) copy-start(f32[32]{0:T(128)} %copy-done.49) | copy-start | bytes 388
  351.1 27.2 %copy-start.65 = (f32[32]{0:T(128)S(1)}, f32[32]{0:T(128)}, u32[]{:S(2)}) copy-start(f32[32]{0:T(128)} %copy-done.64) | copy-start | bytes 388
  442.2 6.5 %copy-start.71 = (bf16[512,2048]{1,0:T(8,128)(2,1)S(1)}, bf16[512,2048]{1,0:T(8,128)(2,1)}, u32[]{:S(2)}) copy-start(bf16[512,2048]{1,0:T(8,128)(2,1)} %copy-done.70) | copy-start | bytes 6291460
  442.2 6.5 %copy-start.73 = (bf16[512,768]{1,0:T(8,128)(2,1)S(1)}, bf16[512,768]{1,0:T(8,128)(2,1)}, u32[]{:S(2)}) copy-start(bf16[512,768]{1,0:T(8,128)(2,1)} %copy-done.72) | copy-start | bytes 2359300
  442.2 11.0 %copy-start.1 = (bf16[1,2048,768]{2,1,0:T(8,128)(2,1)S(1)}, bf16[1,2048,768]{2,1,0:T(8,128)(2,1)}, u32[]{:S(2)}) copy-start(bf16[1,2048,768]{2,1,0:T(8,128)(2,1)} %param.31) | copy-start | bytes 9437188
  (10 other events, 9.1 us)

commit v2 on v1

--- a/solution.py
+++ b/solution.py
@@ -390,12 +390,21 @@
         def _():
             step(self.z + dist)
 
-    def greet(self):
+    def greet(self, plane=False):
         barrier = pltpu.get_barrier_semaphore()
 
         def signal(to):
             pl.semaphore_signal(barrier, inc=1, device_id=self.next_to[to], device_id_type=MESH)
 
+        if plane:
+            groups = self.depth * 2
+            for k in range(1, groups):
+                to = (lax.rem(self.d + k, groups), self.t)
+                pl.semaphore_signal(barrier, inc=1, device_id=to, device_id_type=MESH)
+            signal("y")
+            signal("c")
+            pl.semaphore_wait(barrier, groups + 1)
+            return
         for to in ("x", "y", "c"):
             signal(to)
 
@@ -559,20 +568,20 @@
 class Reduce:
     SEND, RECV = 4 + 4 + 2, 4 + 4 + 2
 
-    def __init__(self, pos, part, core, far, side, column, send, recv):
+    def __init__(self, pos, part, core, far, side, column, send, recv, halves=True):
         self.pos, self.part = pos, part
         self.core, self.far, self.side, self.column = core, far, side, column
         self.send, self.recv = send, recv
         rows = part.shape[1]
-        self.half = (pl.ds(0, rows // 2), pl.ds(rows // 2, rows // 2))
+        self.half = (pl.ds(0, rows // 2), pl.ds(rows // 2, rows // 2)) if halves else (pl.ds(0, rows),)
         self.rounds = pos.depth + 2
 
     @staticmethod
-    def scratch(depth, rows, width):
+    def scratch(depth, rows, width, halves=True):
         b = jnp.bfloat16
         return [
             pltpu.VMEM((depth, 4, rows, width), b),
-            pltpu.VMEM((depth, 2, rows // 2, width), b),
+            pltpu.VMEM((depth, 2, rows // 2, width) if halves else (depth, 1, rows, width), b),
             pltpu.VMEM((depth, 2, rows, width), b),
             pltpu.VMEM((depth, 2, rows, width), b),
             pltpu.SemaphoreType.DMA((Reduce.SEND, depth)),
@@ -619,14 +628,15 @@
             mine = self.core.at[zo, k]
             mine[...] = self.total(mine, self.part.at[self.pos.block(zo, fx, fy)]).astype(mine.dtype)
             if k == 3:
-                self.far_to(zo, 0).start()
-                self.far_to(zo, 1).start()
+                for h in range(len(self.half)):
+                    self.far_to(zo, h).start()
 
     def on_far(self, zo):
         for k in range(2):
-            self.far_to(zo, k).wait_recv()
-            mine = self.core.at[zo, 2 - k, self.half[k]]
-            mine[...] = self.total(mine, self.far.at[zo, k]).astype(mine.dtype)
+            if k < len(self.half):
+                self.far_to(zo, k).wait_recv()
+                mine = self.core.at[zo, 2 - k, self.half[k]]
+                mine[...] = self.total(mine, self.far.at[zo, k]).astype(mine.dtype)
             self.side_to(zo, k).start()
 
     def on_sides(self, zo, mine=False):
@@ -688,8 +698,9 @@
         for fx in range(2):
             for fy in range(2):
                 self.to_core(zo, fx, fy).wait_send()
+        for k in range(len(self.half)):
+            self.far_to(zo, k).wait_send()
         for k in range(2):
-            self.far_to(zo, k).wait_send()
             self.side_to(zo, k).wait_send()
 
         @pl.when(zo < self.pos.z)
@@ -703,6 +714,204 @@
     def end(self):
         for r in range(self.pos.depth):
             self.pos.at(r, self.end_one)
+
+
+class PlaneGather:
+    SEND, RECV = 3, 2
+
+    def __init__(self, pos, own, dst, send, recv):
+        self.pos, self.own, self.dst = pos, own, dst
+        self.send, self.recv = send, recv
+        self.rounds = pos.depth
+
+    def link(self, zo, mine, sends, recvs, to):
+        dst = self.dst(zo * 2 + self.pos.x)
+        return self.pos.copy(self.own if mine else dst, dst, self.send.at[sends, zo], self.recv.at[recvs, zo], to)
+
+    def along_z(self, zo, mine, what):
+        z, depth = self.pos.z, self.pos.depth
+        if mine:
+            up, down = z < depth - 1, z > 0
+        else:
+            up, down = (zo < z) & (z < depth - 1), (zo > z) & (z > 0)
+
+        @pl.when(up)
+        def _():
+            what(self.link(zo, mine, 0, 0, "up"))
+
+        @pl.when(down)
+        def _():
+            what(self.link(zo, mine, 1, 0, "down"))
+
+    def on_column(self, zo, mine=False):
+        if not mine:
+            self.link(zo, False, 0, 0, "up").wait_recv()
+        self.along_z(zo, mine, lambda c: c.start())
+        self.link(zo, mine, 2, 1, "x").start()
+
+    def start(self):
+        self.on_column(self.pos.z, True)
+
+    def round(self, r):
+        if 1 <= r < self.pos.depth:
+            self.pos.at(r, self.on_column)
+
+    def end_one(self, zo, mine=False):
+        across = self.link(zo, mine, 2, 1, "x")
+        across.wait_recv()
+        self.along_z(zo, mine, lambda c: c.wait_send())
+        across.wait_send()
+
+    def end(self):
+        self.end_one(self.pos.z, True)
+        for r in range(1, self.pos.depth):
+            self.pos.at(r, self.end_one)
+
+    @staticmethod
+    def sems(depth):
+        return [pltpu.SemaphoreType.DMA((PlaneGather.SEND, depth)), pltpu.SemaphoreType.DMA((PlaneGather.RECV, depth))]
+
+
+class PlaneReduce:
+    def __init__(self, pos, part, out, across, column, send, recv):
+        self.pos, self.part, self.out = pos, part, out
+        self.across, self.column = across, column
+        self.send, self.recv = send, recv
+        self.rounds = pos.depth
+
+    @staticmethod
+    def scratch(depth, rows, width):
+        b = jnp.bfloat16
+        return [
+            pltpu.VMEM((depth, rows, width), b),
+            pltpu.VMEM((depth, 2, rows, width), b),
+            pltpu.SemaphoreType.DMA((3, depth)),
+            pltpu.SemaphoreType.DMA((3, depth)),
+        ]
+
+    def to_x(self, zo):
+        src = self.part(zo * 2 + 1 - self.pos.x)
+        return self.pos.copy(src, self.across.at[zo], self.send.at[0, zo], self.recv.at[0, zo], "x")
+
+    def down(self, zo):
+        return self.pos.copy(
+            self.across.at[zo], self.column.at[zo, 0], self.send.at[1, zo], self.recv.at[1, zo], "down"
+        )
+
+    def up(self, zo):
+        return self.pos.copy(
+            self.across.at[zo], self.column.at[zo, 1], self.send.at[2, zo], self.recv.at[2, zo], "up"
+        )
+
+    def start(self):
+        for dist in reversed(range(self.pos.depth)):
+            self.pos.at(dist, lambda zo: self.to_x(zo).start())
+
+    def on_column(self, zo):
+        z, depth = self.pos.z, self.pos.depth
+        f32 = jnp.float32
+        here = self.across.at[zo]
+        self.to_x(zo).wait_recv()
+        here[...] = (here[...].astype(f32) + self.part(zo * 2 + self.pos.x)[...].astype(f32)).astype(here.dtype)
+
+        @pl.when((zo < z) & (z < depth - 1))
+        def _():
+            self.down(zo).wait_recv()
+            here[...] = (here[...].astype(f32) + self.column[zo, 0].astype(f32)).astype(here.dtype)
+
+        @pl.when((zo > z) & (z > 0))
+        def _():
+            self.up(zo).wait_recv()
+            here[...] = (here[...].astype(f32) + self.column[zo, 1].astype(f32)).astype(here.dtype)
+
+        @pl.when(zo < z)
+        def _():
+            self.down(zo).start()
+
+        @pl.when(zo > z)
+        def _():
+            self.up(zo).start()
+
+    def on_own(self):
+        z, depth = self.pos.z, self.pos.depth
+        f32 = jnp.float32
+        self.to_x(z).wait_recv()
+        self.out[...] = self.across[z].astype(f32) + self.part(z * 2 + self.pos.x)[...].astype(f32)
+
+        @pl.when(z < depth - 1)
+        def _():
+            self.down(z).wait_recv()
+            self.out[...] += self.column[z, 0].astype(f32)
+
+        @pl.when(z > 0)
+        def _():
+            self.up(z).wait_recv()
+            self.out[...] += self.column[z, 1].astype(f32)
+
+    def round(self, r):
+        dist = self.pos.depth - 1 - r
+        if dist > 0:
+            self.pos.at(dist, self.on_column)
+        elif dist == 0:
+            self.on_own()
+
+    def end_one(self, zo):
+        self.to_x(zo).wait_send()
+
+        @pl.when(zo < self.pos.z)
+        def _():
+            self.down(zo).wait_send()
+
+        @pl.when(zo > self.pos.z)
+        def _():
+            self.up(zo).wait_send()
+
+    def end(self):
+        for r in range(self.pos.depth):
+            self.pos.at(r, self.end_one)
+
+
+class Exchange:
+    def __init__(self, pos, piece, place, send, recv, local):
+        self.pos, self.piece, self.place = pos, piece, place
+        self.send, self.recv, self.local = send, recv, local
+        self.groups = pos.depth * 2
+        self.rounds = 0
+
+    @staticmethod
+    def sems(depth):
+        n = depth * 2 - 1
+        return [pltpu.SemaphoreType.DMA((n,)), pltpu.SemaphoreType.DMA((n,)), pltpu.SemaphoreType.DMA]
+
+    def peer(self, k):
+        return lax.rem(self.pos.d + k, self.groups)
+
+    def copy(self, k):
+        p = self.peer(k)
+        return pltpu.make_async_remote_copy(
+            src_ref=self.piece(p),
+            dst_ref=self.place(self.pos.d),
+            send_sem=self.send.at[k - 1],
+            recv_sem=self.recv.at[k - 1],
+            device_id=(p, self.pos.t),
+            device_id_type=MESH,
+        )
+
+    def here(self):
+        return pltpu.make_async_copy(self.piece(self.pos.d), self.place(self.pos.d), self.local)
+
+    def start(self):
+        self.here().start()
+        for k in range(1, self.groups):
+            self.copy(k).start()
+
+    def round(self, r):
+        pass
+
+    def end(self):
+        self.here().wait()
+        for k in range(1, self.groups):
+            self.copy(k).wait()
 
 
 def drive(*parts):
@@ -783,53 +992,364 @@
     )(part, *blocks)
 
 
-def exchange(groups, number, name, arrays, out_shapes, src_of, dst_of):
-    n = len(arrays)
-
-    def body(*refs):
-        src, out, send, recv, local = refs[:n], refs[n : 2 * n], refs[2 * n], refs[2 * n + 1], refs[2 * n + 2]
-        d = lax.axis_index("dp")
-        t = lax.axis_index("tensor")
-        here = [pltpu.make_async_copy(src_of(i, src[i], d), dst_of(i, out[i], d), local.at[i]) for i in range(n)]
-        for c in here:
+def rows_of(ref, p, rows):
+    return ref.at[pl.ds(p * rows, rows)]
+
+
+def cols_of(ref, p, cols):
+    return ref.at[:, pl.ds(pl.multiple_of(p * cols, cols), cols)]
+
+
+def part_of(ref, p, rows, first, cols):
+    return ref.at[pl.ds(p * rows, rows), pl.ds(first, cols)]
+
+
+def gather_inputs(depth, number, tokens_share, q_weight, k_weight, v_weight):
+    rows, width = tokens_share.shape
+    w_rows, head = k_weight.shape
+
+    def body(tok, wq, wk, wv, all_tok, w_in, *sems):
+        pos = Place(depth)
+        local = [
+            pltpu.make_async_copy(tok, all_tok.at[pos.block(pos.z)], sems[9].at[0]),
+            pltpu.make_async_copy(wk, part_of(w_in, pos.d, w_rows, head, head), sems[9].at[1]),
+            pltpu.make_async_copy(wv, part_of(w_in, pos.d, w_rows, 2 * head, head), sems[9].at[2]),
+        ]
+        for c in local:
             c.start()
-        barrier = pltpu.get_barrier_semaphore()
-        peers = [lax.rem(d + p, groups) for p in range(1, groups)]
-        for p in peers:
-            pl.semaphore_signal(barrier, inc=1, device_id=(p, t), device_id_type=MESH)
-        pl.semaphore_wait(barrier, groups - 1)
-        copies = []
-        for k, p in enumerate(peers):
-            for i in range(n):
-                copies.append(
-                    pltpu.make_async_remote_copy(
-                        src_ref=src_of(i, src[i], p),
-                        dst_ref=dst_of(i, out[i], d),
-                        send_sem=send.at[i, k],
-                        recv_sem=recv.at[i, k],
-                        device_id=(p, t),
-                        device_id_type=MESH,
-                    )
-                )
-                copies[-1].start()
-        for c in copies:
-            c.wait()
-        for c in here:
+        pos.greet(plane=True)
+        drive(
+            PlaneGather(pos, wk, lambda p: part_of(w_in, p, w_rows, head, head), *sems[0:2]),
+            PlaneGather(pos, wv, lambda p: part_of(w_in, p, w_rows, 2 * head, head), *sems[2:4]),
+            Gather(pos, tok, all_tok, *sems[4:6], False),
+            Exchange(pos, lambda p: cols_of(wq, p, head), lambda p: part_of(w_in, p, w_rows, 0, head), *sems[6:9]),
+        )
+        for c in local:
             c.wait()
 
     return pl.pallas_call(
         body,
-        out_shape=out_shapes,
-        in_specs=[pl.BlockSpec(memory_space=HBM)] * n,
-        out_specs=[pl.BlockSpec(memory_space=HBM)] * n,
+        out_shape=[
+            jax.ShapeDtypeStruct((depth * 8, rows, width), tokens_share.dtype),
+            jax.ShapeDtypeStruct((width, 3 * head), q_weight.dtype),
+        ],
+        in_specs=[pl.BlockSpec(memory_space=HBM)] * 4,
+        out_specs=[pl.BlockSpec(memory_space=HBM)] * 2,
+        scratch_shapes=PlaneGather.sems(depth) * 2
+        + Gather.sems(depth)
+        + Exchange.sems(depth)
+        + [pltpu.SemaphoreType.DMA((3,))],
+        compiler_params=params(number),
+        name="gather_inputs",
+    )(tokens_share, q_weight, k_weight, v_weight)
+
+
+def gather_heads(depth, number, routes, out_weight, head):
+    w_rows, width = out_weight.shape[0], out_weight.shape[0] * depth * 2
+
+    def body(route, wo, all_route, w_o, *sems):
+        pos = Place(depth)
+        local = pltpu.make_async_copy(route, all_route.at[pos.block(pos.z)], sems[5])
+        local.start()
+        pos.greet(plane=True)
+        drive(
+            Exchange(pos, lambda p: cols_of(wo, p, head), lambda p: rows_of(w_o, p, w_rows), *sems[2:5]),
+            Gather(pos, route, all_route, *sems[0:2], False),
+        )
+        local.wait()
+
+    return pl.pallas_call(
+        body,
+        out_shape=[
+            jax.ShapeDtypeStruct((depth * 8,) + routes.shape, routes.dtype),
+            jax.ShapeDtypeStruct((width, head), out_weight.dtype),
+        ],
+        in_specs=[pl.BlockSpec(memory_space=HBM)] * 2,
+        out_specs=[pl.BlockSpec(memory_space=HBM)] * 2,
+        scratch_shapes=Gather.sems(depth) + Exchange.sems(depth) + [pltpu.SemaphoreType.DMA],
+        compiler_params=params(number),
+        name="gather_heads",
+    )(routes, out_weight)
+
+
+def dot(a, b):
+    return jnp.dot(a, b, preferred_element_type=jnp.float32)
+
+
+def dot_nt(a, b):
+    return lax.dot_general(a, b, (((1,), (1,)), ((), ())), preferred_element_type=jnp.float32)
+
+
+def dot_tn(a, b):
+    return lax.dot_general(a, b, (((0,), (0,)), ((), ())), preferred_element_type=jnp.float32)
+
+
+def loop(count, step):
+    lax.fori_loop(0, count, lambda i, _: (step(i), 0)[1], 0)
+
+
+def experts(depth, number, normed, out_grad, select, select_t, named, router, w_gate, w_up, w_down):
+    f32, bf = jnp.float32, jnp.bfloat16
+    rows, width = normed.shape
+    devices = depth * 8
+    planes, picks, plane_rows = select.shape
+    slots = planes * picks
+    ff = w_gate.shape[1]
+    lanes = router.shape[1]
+    wide = width + lanes
+    tile = 256
+
+    def body(
+        n_ref, g_ref, sel, sel_t, named_ref, router_ref, wg_hbm, wu_hbm, wd_hbm,
+        out_sum, grad_sum, n_all, x_out, gret_out, inner_out, ggate_out, gup_out,
+        wg, wu, wd, nb, gb, part, xin, gret, ret, inner, ggate, gup, act_a, act_u, gates,
+        w_sem, own_sem, all_sem, keep_sem, *rest,
+    ):
+        pos = Place(depth)
+        expert = pos.block(pos.z)
+        loads = [
+            pltpu.make_async_copy(src, dst, w_sem.at[i])
+            for i, (src, dst) in enumerate(((wg_hbm, wg), (wu_hbm, wu), (wd_hbm, wd)))
+        ]
+        own = [
+            pltpu.make_async_copy(n_ref, nb.at[expert], own_sem.at[0]),
+            pltpu.make_async_copy(g_ref, gb.at[expert], own_sem.at[1]),
+        ]
+        for c in own + loads:
+            c.start()
+        pos.greet()
+        g_normed = Gather(pos, n_ref, nb, *rest[0:2], True)
+        g_grad = Gather(pos, g_ref, gb, *rest[2:4], True)
+        r_out = Reduce(pos, nb, *rest[4:10])
+        r_grad = Reduce(pos, part, *rest[10:16])
+        r_out.out, r_grad.out = out_sum, grad_sum
+
+        def plane(ref, z):
+            return ref[pl.ds(z * 8, 8)].reshape(plane_rows, ref.shape[2])
+
+        def picked(z):
+            return pl.ds(pl.multiple_of(z * picks, picks), picks)
+
+        def cols(i, size=tile):
+            return pl.ds(pl.multiple_of(i * size, size), size)
+
+        here = lax.broadcasted_iota(jnp.int32, (plane_rows, lanes), 1) == expert
+
+        def choose(z):
+            tok = plane(nb, z)
+            logits = dot(tok, router_ref[...])
+            chosen = named_ref[z] > 0
+            top = jnp.max(jnp.where(chosen, logits, -1e30), axis=1, keepdims=True)
+            raised = jnp.where(chosen, jnp.exp(jnp.minimum(logits - top, 0.0)), 0.0)
+            gates[z] = raised / jnp.sum(raised, axis=1, keepdims=True)
+            xin[picked(z), :] = dot(sel[z], tok).astype(bf)
+
+        def forward(i):
+            a = dot(xin[...], wg[:, cols(i)])
+            u = dot(xin[...], wu[:, cols(i)])
+            act_a[:, cols(i)] = a
+            act_u[:, cols(i)] = u
+            inner[:, cols(i)] = (a / (1.0 + jnp.exp(-a)) * u).astype(bf)
+
+        def produce(i):
+            ret[:, cols(i)] = dot(inner[...], wd[:, cols(i)]).astype(bf)
+
+        def spread(z):
+            gate = gates[z]
+            mine = jnp.sum(jnp.where(here, gate, 0.0), axis=1, keepdims=True)
+            summed = jnp.zeros((plane_rows, 1), f32)
+            for i in range(width // 512):
+                c = pl.ds(i * 512, 512)
+                g = gb[pl.ds(z * 8, 8), :, c].reshape(plane_rows, 512).astype(f32)
+                gret[picked(z), c] = dot(sel[z], (mine * g).astype(bf)).astype(bf)
+                back = dot(sel_t[z], ret[picked(z), c])
+                nb[pl.ds(z * 8, 8), :, c] = (mine * back).astype(bf).reshape(8, rows, 512)
+                summed += jnp.sum(g * back, axis=1, keepdims=True)
+            logit = gate * (jnp.where(here, 1.0, 0.0) - mine) * summed
+            part[pl.ds(z * 8, 8), :, pl.ds(width, lanes)] = logit.astype(bf).reshape(8, rows, lanes)
+
+        def backward(i):
+            gi = dot_nt(gret[...], wd[cols(i), :])
+            a = act_a[:, cols(i)]
+            s = 1.0 / (1.0 + jnp.exp(-a))
+            ggate[:, cols(i)] = (gi * act_u[:, cols(i)] * (s + a * s * (1.0 - s))).astype(bf)
+            gup[:, cols(i)] = (gi * (a * s)).astype(bf)
+
+        def inputs_back(i):
+            ret[:, cols(i)] = (dot_nt(ggate[...], wg[cols(i), :]) + dot_nt(gup[...], wu[cols(i), :])).astype(bf)
+
+        def scatter(z):
+            for i in range(width // 512):
+                c = pl.ds(i * 512, 512)
+                part[pl.ds(z * 8, 8), :, c] = dot(sel_t[z], ret[picked(z), c]).astype(bf).reshape(8, rows, 512)
+            r_grad.start_one(z)
+
+        g_normed.start()
+        for r in range(1, 4):
+            g_normed.round(r)
+        g_grad.start()
+        for r in range(4, g_normed.rounds):
+            g_normed.round(r)
+        own[0].wait()
+        g_normed.end()
+        keep = pltpu.make_async_copy(nb, n_all, all_sem)
+        keep.start()
+        g_grad.round(1)
+        loop(planes, choose)
+        g_grad.round(2)
+        loads[0].wait()
+        loads[1].wait()
+        loop(ff // tile, forward)
+        g_grad.round(3)
+        loads[2].wait()
+        loop(width // tile, produce)
+        for r in range(4, g_grad.rounds):
+            g_grad.round(r)
+        own[1].wait()
+        g_grad.end()
+        keep.wait()
+        loop(planes, spread)
+        r_out.start()
+        loop(ff // tile, backward)
+        r_out.round(0)
+        loop(width // tile, inputs_back)
+        r_out.round(1)
+        for dist in reversed(range(depth)):
+            pos.at(dist, scatter)
+        kept = [
+            pltpu.make_async_copy(src, dst, keep_sem.at[i])
+            for i, (src, dst) in enumerate(
+                ((xin, x_out), (gret, gret_out), (inner, inner_out), (ggate, ggate_out), (gup, gup_out))
+            )
+        ]
+        for c in kept:
+            c.start()
+        for r in range(2, r_out.rounds):
+            r_out.round(r)
+            if r >= 3:
+                r_grad.round(r - 3)
+        for r in range(r_out.rounds - 3, r_grad.rounds):
+            r_grad.round(r)
+        for c in kept:
+            c.wait()
+        r_out.end()
+        r_grad.end()
+
+    vmem, hbm = pl.BlockSpec(memory_space=pltpu.VMEM), pl.BlockSpec(memory_space=HBM)
+    dma = pltpu.SemaphoreType.DMA
+    return pl.pallas_call(
+        body,
+        out_shape=[
+            jax.ShapeDtypeStruct((rows, width), f32),
+            jax.ShapeDtypeStruct((rows, wide), f32),
+            jax.ShapeDtypeStruct((devices, rows, width), bf),
+            jax.ShapeDtypeStruct((slots, width), bf),
+            jax.ShapeDtypeStruct((slots, width), bf),
+            jax.ShapeDtypeStruct((slots, ff), bf),
+            jax.ShapeDtypeStruct((slots, ff), bf),
+            jax.ShapeDtypeStruct((slots, ff), bf),
+        ],
+        in_specs=[hbm, hbm] + [vmem] * 4 + [hbm] * 3,
+        out_specs=[vmem, vmem] + [hbm] * 6,
         scratch_shapes=[
-            pltpu.SemaphoreType.DMA((n, groups - 1)),
-            pltpu.SemaphoreType.DMA((n, groups - 1)),
-            pltpu.SemaphoreType.DMA((n,)),
+            pltpu.VMEM((width, ff), bf),
+            pltpu.VMEM((width, ff), bf),
+            pltpu.VMEM((ff, width), bf),
+            pltpu.VMEM((devices, rows, width), bf),
+            pltpu.VMEM((devices, rows, width), bf),
+            pltpu.VMEM((devices, rows, wide), bf),
+            pltpu.VMEM((slots, width), bf),
+            pltpu.VMEM((slots, width), bf),
+            pltpu.VMEM((slots, width), bf),
+            pltpu.VMEM((slots, ff), bf),
+            pltpu.VMEM((slots, ff), bf),
+            pltpu.VMEM((slots, ff), bf),
+            pltpu.VMEM((slots, ff), f32),
+            pltpu.VMEM((slots, ff), f32),
+            pltpu.VMEM((planes, plane_rows, lanes), f32),
+            dma((3,)),
+            dma((2,)),
+            dma,
+            dma((5,)),
+        ]
+        + Gather.sems(depth) * 2
+        + Reduce.scratch(depth, rows, width)
+        + Reduce.scratch(depth, rows, wide),
+        compiler_params=params(number, 60 * 2**20),
+        name="experts",
+    )(normed, out_grad, select, select_t, named, router, w_gate, w_up, w_down)
+
+
+def expert_weight_grads(xin, gret, inner, ggate, gup):
+    f32 = jnp.float32
+    slots, width = xin.shape
+    ff = inner.shape[1]
+    steps = width // 256
+
+    def body(x, g, i, gg, gu, wg, wu, wd):
+        wg[...] = dot_tn(x[...], gg[...])
+        wu[...] = dot_tn(x[...], gu[...])
+        wd[...] = dot_tn(i[...], g[...])
+
+    whole = pl.BlockSpec((slots, ff), lambda s: (0, 0))
+    tall = pl.BlockSpec((slots, 256), lambda s: (0, s))
+    return pl.pallas_call(
+        body,
+        grid=(steps,),
+        out_shape=[jax.ShapeDtypeStruct((width, ff), f32)] * 2 + [jax.ShapeDtypeStruct((ff, width), f32)],
+        in_specs=[tall, tall, whole, whole, whole],
+        out_specs=[pl.BlockSpec((256, ff), lambda s: (s, 0))] * 2 + [pl.BlockSpec((ff, 256), lambda s: (0, s))],
+        compiler_params=pltpu.CompilerParams(vmem_limit_bytes=40 * 2**20),
+        name="expert_weight_grads",
+    )(xin, gret, inner, ggate, gup)
+
+
+def reduce_inputs(depth, number, part, w_part, o_part, small):
+    devices, rows, width = part.shape
+    w_rows, head = w_part.shape[0] // (depth * 2), o_part.shape[1]
+    groups = depth * 2
+    n_red, n_plane = 6, 4
+
+    def body(part_ref, w_ref, o_ref, s_ref, sum_ref, kv_ref, q_ref, out_ref, s_all, *rest):
+        red_scratch, rest = rest[:n_red], rest[n_red:]
+        plane_scratch, rest = rest[:n_plane], rest[n_plane:]
+        pos = Place(depth)
+        local = pltpu.make_async_copy(s_ref, s_all.at[pos.block(pos.z)], rest[8])
+        local.start()
+        pos.greet(plane=True)
+        red = Reduce(pos, part_ref, *red_scratch, halves=False)
+        red.out = sum_ref
+        drive(
+            Exchange(
+                pos, lambda p: part_of(w_ref, p, w_rows, 0, head), lambda p: cols_of(q_ref, p, head), *rest[0:3]
+            ),
+            Exchange(pos, lambda p: rows_of(o_ref, p, w_rows), lambda p: cols_of(out_ref, p, head), *rest[3:6]),
+            red,
+            PlaneReduce(pos, lambda p: part_of(w_ref, p, w_rows, head, 2 * head), kv_ref, *plane_scratch),
+            Gather(pos, s_ref, s_all, *rest[6:8], False),
+        )
+        local.wait()
+
+    vmem, hbm = pl.BlockSpec(memory_space=pltpu.VMEM), pl.BlockSpec(memory_space=HBM)
+    return pl.pallas_call(
+        body,
+        out_shape=[
+            jax.ShapeDtypeStruct((rows, width), jnp.float32),
+            jax.ShapeDtypeStruct((w_rows, 2 * head), jnp.float32),
+            jax.ShapeDtypeStruct((w_rows, groups * head), w_part.dtype),
+            jax.ShapeDtypeStruct((w_rows, groups * head), w_part.dtype),
+            jax.ShapeDtypeStruct((devices,) + small.shape, small.dtype),
         ],
-        compiler_params=params(number),
-        name=name,
-    )(*arrays)
+        in_specs=[vmem, vmem, hbm, hbm],
+        out_specs=[vmem, vmem, hbm, hbm, hbm],
+        scratch_shapes=Reduce.scratch(depth, rows, width, False)
+        + PlaneReduce.scratch(depth, w_rows, 2 * head)
+        + Exchange.sems(depth) * 2
+        + Gather.sems(depth)
+        + [pltpu.SemaphoreType.DMA],
+        compiler_params=params(number, 48 * 2**20),
+        name="reduce_inputs",
+    )(part, w_part, o_part, small)
 
 
 def head_shards(
@@ -874,33 +1394,14 @@
 
     tokens_share = lax.dynamic_slice_in_dim(tokens, lane * share_rows, share_rows, 0)
     routes_block = jnp.zeros((8, 128), jnp.int32).at[: share_rows * top_count // 128].set(routes.reshape(-1, 128))
-    all_tok, all_routes = all_gather(depth, 0, "gather_tokens", tokens_share, routes_block)
+    all_tok, w_in = gather_inputs(depth, 0, tokens_share, q_weight, k_weight, v_weight)
     all_tok = all_tok.reshape(all_tokens, width)
+    all_routes, w_o = gather_heads(depth, 1, routes_block, out_weight, head_dim)
     all_routes = all_routes[:, : share_rows * top_count // 128].reshape(all_tokens, top_count)
-
-    def rows_of(ref, p):
-        return ref.at[pl.ds(p * weight_rows, weight_rows)]
-
-    def cols_of(ref, p):
-        return ref.at[:, pl.ds(pl.multiple_of(p * head_dim, head_dim), head_dim)]
-
-    head_weight = jax.ShapeDtypeStruct((width, head_dim), bf)
-    w_q, w_o, w_k, w_v = exchange(
-        groups,
-        1,
-        "exchange_weights",
-        [q_weight, out_weight, k_weight, v_weight],
-        [head_weight] * 4,
-        lambda i, ref, p: cols_of(ref, p) if i < 2 else ref,
-        lambda i, ref, p: rows_of(ref, p),
-    )
-    (all_grad,) = all_gather(depth, 2, "gather_out_grad", out_grad)
-    all_grad = all_grad.reshape(all_tokens, width)
 
     tok_float = all_tok.astype(f32)
     norm_gain_float = norm_gain.astype(f32)
     hidden = norm_rows(tok_float, norm_gain_float).astype(bf)
-    w_in = jnp.concatenate([w_q, w_k, w_v], axis=1)
     projected = jnp.dot(hidden, w_in, preferred_element_type=f32)
 
     def prepare_local(projected_in, qgain_in, kgain_in):
@@ -925,65 +1426,44 @@
 
     middle = tokens_share.astype(f32) + branch
     normed_float, moe_norm_back = jax.vjp(norm_rows, middle, moe_gain.astype(f32))
-    (normed,) = all_gather(depth, 4, "gather_normed", normed_float.astype(bf))
-    normed = normed.reshape(all_tokens, width)
-    logits = jnp.dot(normed, router_weight, preferred_element_type=f32)
-    named = jnp.any(all_routes[:, :, None] == jnp.arange(expert_count, dtype=jnp.int32), axis=1)
-
-    probabilities = jax.nn.softmax(logits, axis=-1)
-    chosen = jnp.where(named, probabilities, 0.0)
-    gate_all = chosen / jnp.sum(chosen, axis=1, keepdims=True)
-    here = jnp.arange(expert_count, dtype=jnp.int32) == expert
-    mine = jnp.any(named & here, axis=1)
-    gate_mine = jnp.sum(jnp.where(here, gate_all, 0.0), axis=1)
-    rank = jnp.cumsum(mine.astype(jnp.int32)) - 1
-    select = ((rank[None, :] == jnp.arange(slots, dtype=jnp.int32)[:, None]) & mine[None, :]).astype(bf)
-    inputs = jnp.dot(select, normed, preferred_element_type=f32).astype(bf)
-    grads = jnp.dot(select, all_grad, preferred_element_type=f32)
-    gate_rows = jnp.sum(jnp.where(select > 0, gate_mine[None, :], 0.0), axis=1)
-    w_gate, w_up, w_down = gate_weight[0], up_weight[0], down_weight[0]
-    gate_act = jnp.dot(inputs, w_gate, preferred_element_type=f32)
-    up_act = jnp.dot(inputs, w_up, preferred_element_type=f32)
-    inner_float, swiglu_back = jax.vjp(swiglu, gate_act, up_act)
-    inner_act = inner_float.astype(bf)
-    returned = jnp.dot(inner_act, w_down, preferred_element_type=f32).astype(bf)
-    grad_returned = (gate_rows[:, None] * grads).astype(bf)
-    grad_gate_rows = jnp.sum(grads * returned.astype(f32), axis=1)
-    out_rows = (gate_rows[:, None] * returned.astype(f32)).astype(bf)
-    out_part = jnp.einsum("rt,rd->td", select, out_rows, preferred_element_type=f32).astype(bf)
-    (out_sum,) = reduce_scatter(
-        depth, 5, "reduce_out", out_part.reshape(expert_count, share_rows, width)
-    )
+    plane_rows = all_tokens // depth
+    picks = slots // depth
+    lanes = 128
+    mine = jnp.any(all_routes == expert, axis=1).reshape(depth, plane_rows)
+    rank = jnp.cumsum(mine.astype(jnp.int32), axis=1) - 1
+    pick = jnp.arange(picks, dtype=jnp.int32)
+    select = ((rank[:, None, :] == pick[None, :, None]) & mine[:, None, :]).astype(bf)
+    select_t = ((rank[:, :, None] == pick[None, None, :]) & mine[:, :, None]).astype(bf)
+    named = jnp.any(all_routes[:, :, None] == jnp.arange(lanes, dtype=jnp.int32), axis=1).astype(f32)
+    router = jnp.pad(router_weight, ((0, 0), (0, lanes - expert_count)))
+    out_sum, grad_sum, all_normed, *kept = experts(
+        depth,
+        4,
+        normed_float.astype(bf),
+        out_grad,
+        select,
+        select_t,
+        named.reshape(depth, plane_rows, lanes),
+        router,
+        gate_weight[0],
+        up_weight[0],
+        down_weight[0],
+    )
+    grad_gate_w, grad_up_w, grad_down = expert_weight_grads(*kept)
     layer_out = (middle + out_sum).astype(bf)
-    grad_inner = jnp.einsum("rd,fd->rf", grad_returned, w_down, preferred_element_type=f32)
-    grad_down = jnp.einsum("rf,rd->fd", inner_act, grad_returned, preferred_element_type=f32)
-    grad_gate_float, grad_up_float = swiglu_back(grad_inner)
-    grad_gate_act = grad_gate_float.astype(bf)
-    grad_up_act = grad_up_float.astype(bf)
-    grad_gate_w = jnp.einsum("rd,rf->df", inputs, grad_gate_act, preferred_element_type=f32)
-    grad_up_w = jnp.einsum("rd,rf->df", inputs, grad_up_act, preferred_element_type=f32)
-    grad_inputs = jnp.einsum("rf,df->rd", grad_gate_act, w_gate, preferred_element_type=f32)
-    grad_inputs = (
-        grad_inputs + jnp.einsum("rf,df->rd", grad_up_act, w_up, preferred_element_type=f32)
-    ).astype(bf)
-    grad_gate_mine = jnp.sum(jnp.where(select > 0, grad_gate_rows[:, None], 0.0), axis=0)
-    own_grad = jnp.where(here, grad_gate_mine[:, None], 0.0)
-    own_logit_grad = gate_all * (own_grad - jnp.sum(gate_all * own_grad, axis=1, keepdims=True))
-    normed_part = jnp.einsum("rt,rd->td", select, grad_inputs, preferred_element_type=f32) + jnp.einsum(
-        "te,de->td", own_logit_grad.astype(bf), router_weight, preferred_element_type=f32
-    )
-    (grad_normed,) = reduce_scatter(
-        depth, 6, "reduce_normed", normed_part.astype(bf).reshape(expert_count, share_rows, width)
-    )
+    logit_grad = grad_sum[:, width:].astype(bf)
+    grad_normed = grad_sum[:, :width] + jnp.einsum("te,de->td", logit_grad, router, preferred_element_type=f32)
     grad_middle_part, grad_moe_gain = moe_norm_back(grad_normed)
     grad_middle = out_grad.astype(f32) + grad_middle_part
-    all_branch, all_gate_grads = all_gather(
-        depth, 7, "gather_grad_branch", grad_middle.astype(bf), grad_gate_mine.reshape(8, -1)
-    )
-    grad_branch = all_branch.reshape(all_tokens, width)
-    gate_grads = all_gate_grads.reshape(expert_count, all_tokens).T
-    logit_grads = gate_all * (gate_grads - jnp.sum(gate_all * gate_grads, axis=1, keepdims=True))
-    grad_router = jnp.einsum("td,te->de", normed, logit_grads.astype(bf), preferred_element_type=f32)
+    (all_branch,) = all_gather(
+        depth, 7, "gather_grad_branch", jnp.concatenate([grad_middle.astype(bf), logit_grad], axis=1)
+    )
+    all_branch = all_branch.reshape(all_tokens, width + lanes)
+    grad_branch = all_branch[:, :width]
+    grad_router = jnp.einsum(
+        "td,te->de", all_normed.reshape(all_tokens, width), all_branch[:, width : width + expert_count],
+        preferred_element_type=f32,
+    )
 
     grad_heads = jnp.dot(grad_branch, w_o, preferred_element_type=f32).astype(bf)
     out_weight_part = jnp.einsum("td,tc->dc", grad_branch, attended, preferred_element_type=f32).astype(bf)
@@ -1005,23 +1485,12 @@
     small = jnp.concatenate([grad_norm_gain, grad_moe_gain, grad_q_gain, grad_k_gain])
     small_rows = -(-small.shape[0] // 1024) * 8
     small_block = jnp.pad(small, (0, small_rows * 128 - small.shape[0])).reshape(small_rows, 128)
-    grad_hidden, all_small = reduce_scatter(
-        depth, 8, "reduce_hidden", hidden_part.astype(bf).reshape(expert_count, share_rows, width), small_block
+    grad_hidden, kv_sum, grad_q, grad_o, all_small = reduce_inputs(
+        depth, 8, hidden_part.astype(bf).reshape(expert_count, share_rows, width), in_weight_part, out_weight_part, small_block
     )
     _, share_norm_back = jax.vjp(norm_rows, tokens_share.astype(f32), norm_gain_float)
     tokens_grad = grad_middle + share_norm_back(grad_hidden)[0]
     small_sums = jnp.sum(all_small, axis=0).reshape(-1)
-    grad_q, grad_o, grad_kv = exchange(
-        groups,
-        9,
-        "exchange_weight_grads",
-        [in_weight_part[:, :head_dim], out_weight_part, in_weight_part[:, head_dim:]],
-        [jax.ShapeDtypeStruct(q_weight.shape, bf)] * 2
-        + [jax.ShapeDtypeStruct((groups, weight_rows, 2 * head_dim), bf)],
-        lambda i, ref, p: rows_of(ref, p),
-        lambda i, ref, p: cols_of(ref, p) if i < 2 else ref.at[p],
-    )
-    kv_sum = jnp.sum(grad_kv.astype(f32), axis=0)
     return (
         layer_out,
         tokens_grad,

time: 461 us -> 381 us (0.83)
  the two profiles are of different devices: /device:TPU:11 before, /device:TPU:0 now
where the time goes in v2:
time: 381 us; the launch traced here: 376 us
  Pallas kernels  292 us (77%)
  other arithmetic  40.3 us (11%)
  matrix products  25.7 us (7%)
  local copies, waits for them, and re-layouts  16.5 us (4%)
    pallas_call x1, Pallas kernels, experts(): pl.pallas_call(body, out_shape=[jax.ShapeDtypeStruct((rows, width), f32),...  97.9 us
    pallas_call x1, Pallas kernels, reduce_inputs(): pl.pallas_call(body, out_shape=[jax.ShapeDtypeStruct((rows, width), jnp.f...  55.4 us
    pallas_call x1, Pallas kernels, gather_inputs(): pl.pallas_call(body, out_shape=[jax.ShapeDtypeStruct((depth * 8, rows, wi...  43.4 us
    pallas_call x1, Pallas kernels, gather_heads(): pl.pallas_call(body, out_shape=[jax.ShapeDtypeStruct((depth * 8,) + route...  32.4 us
    pallas_call x1, Pallas kernels, all_gather(): pl.pallas_call(body, out_shape=[jax.ShapeDtypeStruct((depth * 8,) + b.sha...  28.7 us
    pallas_call x1, Pallas kernels, reduce_scatter(): pl.pallas_call(body, out_shape=[jax.ShapeDtypeStruct((rows, width), jnp.f...  24.8 us
    pallas_call x1, Pallas kernels, expert_weight_grads(): pl.pallas_call(body, grid=(steps,), out_shape=[jax.ShapeDtypeStruct((widt...  9.1 us

profile of v2, /device:TPU:0, one launch (start us, length us, event | category | flops | bytes accessed | tf_op | source)
XLA Modules:
  0.0 376.0 jit_solution(15231717500719965592)
XLA Ops:
  0.7 0.7 convert_element_type.132
  1.3 0.7 convert_element_type.135
  2.0 0.8 slice_compare_fusion
  3.5 0.7 convert_element_type.139
  4.2 0.7 convert_element_type.130
  4.9 0.8 copy.42
  5.7 0.6 scatter.4.route
  6.3 1.6 constant_dynamic-slice_fusion.tok
  7.9 1.2 copy.45
  9.1 0.9 pad.32.router_ref
  10.0 32.4 %gather_heads.1 = (s32[32,8,128]{2,1,0:T(8,128)}, bf16[2048,128]{1,0:T(8,128)(2,1)}) custom-call(s32[8,128]{1,0:T(8,128)} %scatter.4.route, bf16[256,1024]{1,0:T(8,128)(2,1)} %wo.1), custom_call_target="tpu_custom_call" | custom-call | tf_op jit(solution)/shard_map/gather_heads/pallas_call | solution.py:1061
  42.4 0.9 slice.114
  43.3 0.3 reshape.393
  43.8 5.8 %fusion.1 = pred[1024,128]{1,0:T(8,128)(4,1)S(1)} fusion(s32[1024,8]{1,0:T(8,128)S(1)} %reshape.393), kind=kLoop, calls=%fused_computation.10 | loop fusion | flops 1966080 | bytes 163840 | tf_op jit(solution)/shard_map/reduce_or | solution.py:1437
  49.6 1.2 reduce-window.19
  51.3 1.0 fusion.30.sel_t
  52.3 0.8 fusion.28.sel
  53.1 0.8 convert_element_type.162
  53.9 43.4 %gather_inputs.1 = (bf16[32,32,2048]{2,1,0:T(8,128)(2,1)}, bf16[2048,384]{1,0:T(8,128)(2,1)}) custom-call(bf16[32,2048]{1,0:T(8,128)(2,1)} %constant_dynamic-slice_fusion.tok, bf16[256,1024]{1,0:T(8,128)(2,1)} %wq.1, bf16[256,128]{1,0:T(8,128)(2,1)} %wk.1, bf16[256,128]{1,0:T(8,128)(2,1)} %wv.1), custom_call_target="tpu_custom_call" | custom-call | tf_op jit(solution)/shard_map/gather_inputs/pallas_call | solution.py:1030
  97.3 3.1 multiply_reduce_fusion.1
  100.5 3.3 multiply_convert_fusion
  103.9 1.9 fusion.88
  106.0 0.6 copy-done.32
  106.8 1.2 fusion.69
  108.0 1.2 fusion.54
  109.2 1.0 fusion.84
  110.2 1.7 fusion.2
  112.0 0.6 log_add_fusion
  112.6 1.1 fusion.17
  113.7 1.3 convolution_convert_fusion
  115.0 24.8 %reduce_branch.1 = f32[32,2048]{1,0:T(8,128)S(1)} custom-call(bf16[32,32,2048]{2,1,0:T(8,128)(2,1)S(1)} %bitcast.73), custom_call_target="tpu_custom_call" | custom-call | tf_op jit(solution)/shard_map/reduce_branch/pallas_call | solution.py:983
  139.8 1.1 multiply_reduce_fusion.9
  140.8 0.7 multiply_convert_fusion.2.n_ref
  141.6 97.9 %experts.1 = (f32[32,2048]{1,0:T(8,128)}, f32[32,2176]{1,0:T(8,128)}, bf16[32,32,2048]{2,1,0:T(8,128)(2,1)}, bf16[512,2048]{1,0:T(8,128)(2,1)}, bf16[512,2048]{1...) custom-call(bf16[32,2048]{1,0:T(8,128)(2,1)} %multiply_convert_fusion.2.n_ref, ...), custom_call_target="tpu_custom_call" | custom-call | tf_op jit(solution)/shard_map/experts/pallas_call | solution.py:1240
  239.5 1.9 multiply_reduce_fusion.7
  241.4 0.8 slice.195
  242.3 0.7 pad_maximum_fusion.6.refs_0_
  243.0 28.7 %gather_grad_branch.1 = bf16[32,32,2176]{2,1,0:T(8,128)(2,1)} custom-call(bf16[32,2176]{1,0:T(8,128)(2,1)} %pad_maximum_fusion.6.refs_0_), custom_call_target="tpu_custom_call" | custom-call | tf_op jit(solution)/shard_map/gather_grad_branch/pallas_call | solution.py:948
  271.7 3.9 %fusion.63 = f32[2048,32]{0,1:T(8,128)} fusion(bf16[1024,2048]{1,0:T(8,128)(2,1)} %bitcast.74, bf16[1024,2176]{1,0:T(8,128)(2,1)} %bitcast.75), kind=kOutput, calls=%fused_computation.98 | convolution fusion | flops 134217728 | bytes 4718592 | tf_op jit(solution)/shard_map/td,te->de/dot_general | solution.py:1463
  275.6 1.5 multiply_reduce_fusion.4
  277.2 1.3 fusion.9.o_ref
  278.5 0.8 copy-done.14
  279.4 0.9 fusion.15
  280.3 2.4 multiply_convert_fusion.1
  282.8 0.5 fusion.20
  283.3 0.8 convolution_multiply_fusion.1
  284.1 1.2 fusion.57
  285.3 1.2 fusion.51
  287.3 2.5 convolution_convert_fusion.1.w_ref
  290.0 4.8 %multiply_reduce_fusion = (f32[2048]{0:T(1024)S(1)}, bf16[1024,2048]{1,0:T(8,128)(2,1)}) fusion(bf16[32,32,2048]{2,1,0:T(8,128)(2,1)S(1)} %copy-done.8, f32[1024]{0:T(1024)S(1)} %copy-done.38, bf16[2048,384]{1,0:T(8,128)(2,1)S(1)} %copy-done.49, f32[1024,128]{0,1:T(8,128)S(1)} %fusion.24, f32[1024,128]{0,1:T(8,128)S(1)} %add_add_fusion.1, ...), kind=kOutput, calls=%fused_computation.1 | convolution fusion | flops 1622276096 | bytes 11546624 | tf_op jit(solution)/shard_map/tc,dc->td/dot_general | solution.py:1480
  294.7 55.4 %reduce_inputs.1 = (f32[32,2048]{1,0:T(8,128)S(1)}, f32[256,256]{1,0:T(8,128)S(1)}, bf16[256,1024]{1,0:T(8,128)(2,1)S(1)}, bf16[256,1024]{1,0:T(8,128)(2,1)S(1)}, f32[32,40,128]{2,1,0:T(8,128)S(1)}) custom-call(bf16[32,32,2048]{2,1,0:T(8,128)(2,1)} %bitcast.78, bf16[2048,384]{1,0:T(8,128)(2,1)S(1)} %convolution_convert_fusion.1.w_ref, ...), custom_call_target="tpu_custom_call" | custom-call | tf_op jit(solution)/shard_map/reduce_inputs/pallas_call | solution.py:1334
  350.1 0.8 copy-done.5
  351.0 0.8 copy-done.6
  351.8 0.8 copy-done.7
  352.6 1.9 reduce_sum.167
  354.5 1.4 slice_bitcast_fusion.2
  355.8 1.3 slice_bitcast_fusion
  357.1 1.1 fusion.61
  358.2 2.1 fusion.60
  360.3 0.7 fusion.85
  361.0 2.1 convert_element_type.158
  363.1 2.1 convert_element_type.159
  365.3 1.1 copy-done.4
  366.4 9.1 %expert_weight_grads.1 = (f32[2048,768]{1,0:T(8,128)}, f32[2048,768]{1,0:T(8,128)}, f32[768,2048]{1,0:T(8,128)}) custom-call(bf16[512,2048]{1,0:T(8,128)(2,1)S(1)} %copy-done, bf16[512,2048]{1,0:T(8,128)(2,1)S(1)} %copy-done.1, bf16[512,768]{1,0:T(8,128)(2,1)S(1)} %copy-done.2, bf16[512,768]{1,0:T(8,128)(2,1)S(1)} %copy-done.3, bf16[512,768]{1,0:T(8,128)(2,1)S(1)} %copy-done.4), custom_call_target="tpu_custom_call" | custom-call | tf_op jit(solution)/shard_map/expert_weight_grads/pallas_call | solution.py:1296
  (128 shorter events, 3.1 us)
Async XLA Ops:
  0.7 107.3 %copy-start.40 = (f32[64]{0:T(128)}, f32[64]{0:T(128)S(1)}, u32[]{:S(2)}) copy-start(f32[64]{0:T(128)S(1)} %multiply_power_fusion) | copy-start | bytes 772
  1.3 105.2 %copy-start.42 = (f32[128]{0:T(128)}, f32[128]{0:T(128)S(1)}, u32[]{:S(2)}) copy-start(f32[128]{0:T(128)S(1)} %convert_element_type.132) | copy-start | bytes 1540
  2.0 104.6 %copy-start.44 = (f32[128]{0:T(128)}, f32[128]{0:T(128)S(1)}, u32[]{:S(2)}) copy-start(f32[128]{0:T(128)S(1)} %convert_element_type.135) | copy-start | bytes 1540
  3.5 104.5 %copy-start.24 = (f32[1024]{0:T(1024)}, f32[1024]{0:T(1024)S(1)}, u32[]{:S(2)}) copy-start(f32[1024]{0:T(1024)S(1)} %fusion.71) | copy-start | bytes 12292
  100.5 3.3 copy-start.37
  100.5 3.4 copy-start.48
  103.8 2.0 copy-start.11
  105.9 3.3 copy-start.30
  106.0 0.6 copy-start.32
  106.0 4.2 %copy-start.34 = (f32[1024]{0:T(1024)}, f32[1024]{0:T(1024)S(1)}, u32[]{:S(2)}) copy-start(f32[1024]{0:T(1024)S(1)} %get-tuple-element.71) | copy-start | bytes 12292
  106.6 3.6 copy-start.26
  106.6 3.6 copy-start.28
  108.0 2.3 copy-start.18
  109.2 2.8 copy-start.20
  109.2 2.8 copy-start.22
  110.2 2.3 copy-start.13
  112.6 1.1 copy-start.17
  140.8 101.4 %copy-start.9 = (f32[32,2048]{1,0:T(8,128)}, f32[32,2048]{1,0:T(8,128)S(1)}, u32[]{:S(2)}) copy-start(f32[32,2048]{1,0:T(8,128)S(1)} %get-tuple-element.77) | copy-start | bytes 786436
  140.8 101.3 %copy-start.39 = (f32[32]{0:T(128)}, f32[32]{0:T(128)S(1)}, u32[]{:S(2)}) copy-start(f32[32]{0:T(128)S(1)} %fusion.74) | copy-start | bytes 388
  141.6 100.6 %copy-start.16 = (bf16[32,2048]{1,0:T(8,128)(2,1)S(1)}, bf16[32,2048]{1,0:T(8,128)(2,1)}, u32[]{:S(2)}) copy-start(bf16[32,2048]{1,0:T(8,128)(2,1)} %g_ref.1) | copy-start | bytes 393220
  241.4 0.9 copy-start.15
  241.4 0.9 copy-start.47
  271.7 3.9 %copy-start.10 = (bf16[32,32,2176]{2,1,0:T(8,128)(2,1)S(1)}, bf16[32,32,2176]{2,1,0:T(8,128)(2,1)}, u32[]{:S(2)}) copy-start(bf16[32,32,2176]{2,1,0:T(8,128)(2,1)} %gather_grad_branch.1) | copy-start | bytes 13369348
  277.2 2.2 copy-start.14
  277.2 2.2 copy-start.31
  277.2 2.2 copy-start.46
  280.3 2.4 copy-start.21
  280.3 2.4 copy-start.23
  280.3 3.0 copy-start.19
  282.7 1.4 copy-start.25
  282.7 1.4 copy-start.41
  282.7 3.8 %copy-start.29 = (f32[1024]{0:T(1024)S(1)}, f32[1024]{0:T(1024)}, u32[]{:S(2)}) copy-start(f32[1024]{0:T(1024)} %copy-done.28) | copy-start | bytes 12292
  282.7 3.8 %copy-start.45 = (f32[128]{0:T(128)S(1)}, f32[128]{0:T(128)}, u32[]{:S(2)}) copy-start(f32[128]{0:T(128)} %copy-done.44) | copy-start | bytes 1540
  282.8 4.0 %copy-start.27 = (f32[1024]{0:T(1024)S(1)}, f32[1024]{0:T(1024)}, u32[]{:S(2)}) copy-start(f32[1024]{0:T(1024)} %copy-done.26) | copy-start | bytes 12292
  282.8 3.9 %copy-start.43 = (f32[128]{0:T(128)S(1)}, f32[128]{0:T(128)}, u32[]{:S(2)}) copy-start(f32[128]{0:T(128)} %copy-done.42) | copy-start | bytes 1540
  283.2 3.7 copy-start.33
  283.3 3.7 copy-start.35
  284.1 3.1 copy-start.12
  287.3 2.5 copy-start.8
  287.3 2.5 copy-start.38
  287.3 2.7 copy-start.49
  290.0 4.8 %copy-start.36 = (f32[2048]{0:T(1024)S(1)}, f32[2048]{0:T(1024)}, u32[]{:S(2)}) copy-start(f32[2048]{0:T(1024)} %get-tuple-element.72) | copy-start | bytes 24580
  350.1 0.8 copy-start.5
  351.0 0.8 copy-start.6
  351.8 0.8 copy-start.7
  352.5 12.7 %copy-start = (bf16[512,2048]{1,0:T(8,128)(2,1)S(1)}, bf16[512,2048]{1,0:T(8,128)(2,1)}, u32[]{:S(2)}) copy-start(bf16[512,2048]{1,0:T(8,128)(2,1)} %get-tuple-element.58.x) | copy-start | bytes 6291460
  352.5 12.7 %copy-start.2 = (bf16[512,768]{1,0:T(8,128)(2,1)S(1)}, bf16[512,768]{1,0:T(8,128)(2,1)}, u32[]{:S(2)}) copy-start(bf16[512,768]{1,0:T(8,128)(2,1)} %get-tuple-element.60.i) | copy-start | bytes 2359300
  354.4 10.8 %copy-start.1 = (bf16[512,2048]{1,0:T(8,128)(2,1)S(1)}, bf16[512,2048]{1,0:T(8,128)(2,1)}, u32[]{:S(2)}) copy-start(bf16[512,2048]{1,0:T(8,128)(2,1)} %get-tuple-element.59.g) | copy-start | bytes 6291460
  354.4 10.8 %copy-start.3 = (bf16[512,768]{1,0:T(8,128)(2,1)S(1)}, bf16[512,768]{1,0:T(8,128)(2,1)}, u32[]{:S(2)}) copy-start(bf16[512,768]{1,0:T(8,128)(2,1)} %get-tuple-element.61.gg) | copy-start | bytes 2359300
  365.3 1.1 copy-start.4
